TPU v7x, 128 devices: a whole 4x4x4 slice. The times are simulated.
128 devices in a mesh: branch: 2 (over y_hi), res: 64 (over y_lo, z, x, core).
Axes of the slice: x: 4, y: 4 (y_hi: 2, y_lo: 2; y = y_hi * 2 + y_lo), z: 4, core: 2. Of those that a mesh axis runs over, the one named last changes fastest.
Arguments:
- homolog_activations: bfloat16 [64, 1024, 256], P(None, ('branch', 'res')), may hold values from -6 to 6
- standardize_multiplier: float32 [256], replicated, may hold values from 0.5 to 1.5
- first_factor_matrix: bfloat16 [256, 32], replicated, may hold values from -0.375 to 0.375
- second_factor_matrix: bfloat16 [256, 32], replicated, may hold values from -0.375 to 0.375
- final_matrix: bfloat16 [1024, 128], replicated, may hold values from -1.5 to 1.5
- final_offset: float32 [128], replicated, may hold values from -3 to 3
- same_molecule_offset: float32 [128], replicated, may hold values from -3 to 3
- edge_activations: bfloat16 [1024, 1024, 128], P(('branch', 'res')), may hold values from -6 to 6
- edge_result_sensitivity: bfloat16 [1024, 1024, 128], P(('branch', 'res')), may hold values from -24 to 24
- padding_indicator: int32 [1024], P(('branch', 'res')), may hold values from 0 to 1, as said below
- molecule_identity: int32 [1024], P(('branch', 'res')), may hold values from 0 to 63, as said below
Outputs:
- updated_pair_state: bfloat16 [1024, 1024, 128], P(('branch', 'res'))
- alignment_gradient: float32 [64, 1024, 256], P(None, ('branch', 'res'))
Inputs may be any that keep to these rules, and one draw needn't show every extreme that they name: `padding_indicator`: 1 on the first 512 residues; each of the last 512 residues has its own value, 0 or 1, and the last residue is 0. `molecule_identity`: never falls along the residues; each chain is a run of residues.
All inputs are finite; a program needn't handle non-finite values.
Results may differ from a plain program's by a relative error of at most 0.0064.
Values may be sent and summed in bfloat16 or wider, within the bound.
A program may use at most 192 MiB of HBM per device.

v0:
```python
import jax
import jax.numpy as jnp
from jax import lax
from jax.sharding import PartitionSpec as P

HOMOLOG_COUNT = 64
FACTOR_WIDTH = 32


EPSILON = 1e-05


def moment_summary(homolog_activations, standardize_multiplier):
    contribution_sequences = homolog_activations.astype(jnp.float32)
    centred = contribution_sequences - jnp.mean(contribution_sequences, axis=-1, keepdims=True)
    averaged_result = lax.rsqrt(jnp.mean(centred * centred, axis=-1, keepdims=True) + EPSILON)
    whitened_features = centred * averaged_result
    return (
        whitened_features,
        averaged_result,
        (whitened_features * standardize_multiplier).astype(jnp.bfloat16),
    )


def local(
    homolog_activations,
    standardize_multiplier,
    first_factor_matrix,
    second_factor_matrix,
    final_matrix,
    final_offset,
    same_molecule_offset,
    edge_activations,
    edge_result_sensitivity,
    padding_indicator,
    molecule_identity,
):
    whitened_features, averaged_result, standardized_features = moment_summary(
        homolog_activations, standardize_multiplier
    )
    first_factor = jnp.dot(
        standardized_features, first_factor_matrix, preferred_element_type=jnp.float32
    ).astype(jnp.bfloat16)
    right = jnp.dot(
        standardized_features, second_factor_matrix, preferred_element_type=jnp.float32
    ).astype(jnp.bfloat16)
    labels = lax.all_gather(
        jnp.stack([padding_indicator, molecule_identity]), ("branch", "res"), axis=1, tiled=True
    )
    keep_all = labels[0].astype(jnp.float32)
    chain_all = labels[1]
    keep_own = padding_indicator.astype(jnp.float32)
    right_all = lax.all_gather(right, ("branch", "res"), axis=1, tiled=True)
    total = right_all.shape[1]
    weight_mask = keep_own[:, None] * keep_all[None, :]
    same = (molecule_identity[:, None] == chain_all[None, :]).astype(jnp.float32)
    first_factor_sequences = jnp.transpose(first_factor, (1, 0, 2))

    def row_step(running_total, pieces):
        left_row, pair_row, cot_row, mask_row, same_row = pieces
        tensor_product = (
            jnp.einsum("sa,sjb->jab", left_row, right_all, preferred_element_type=jnp.float32)
            / HOMOLOG_COUNT
        ).astype(jnp.bfloat16)
        project = jnp.dot(
            tensor_product.reshape(total, FACTOR_WIDTH * FACTOR_WIDTH),
            final_matrix,
            preferred_element_type=jnp.float32,
        )
        update = mask_row[:, None] * (
            project + final_offset + same_row[:, None] * same_molecule_offset
        )
        new_row = (pair_row.astype(jnp.float32) + update).astype(jnp.bfloat16)
        reverse_sweep = (
            jnp.dot(cot_row, final_matrix.T, preferred_element_type=jnp.float32) * mask_row[:, None]
        ).astype(jnp.bfloat16)
        return (running_total, (new_row, reverse_sweep.reshape(total, FACTOR_WIDTH, FACTOR_WIDTH)))

    _, (updated_pair_state, reverse_sweep_full) = lax.scan(
        row_step,
        jnp.float32(0),
        (first_factor_sequences, edge_activations, edge_result_sensitivity, weight_mask, same),
    )
    sensitivity_first_factor = (
        jnp.einsum(
            "prut,ort->opu", reverse_sweep_full, right_all, preferred_element_type=jnp.float32
        )
        / HOMOLOG_COUNT
    )
    partial_terms = (
        jnp.einsum(
            "fctr,nft->ncr", reverse_sweep_full, first_factor, preferred_element_type=jnp.float32
        )
        / HOMOLOG_COUNT
    )
    grad_right = lax.psum_scatter(partial_terms, ("branch", "res"), scatter_dimension=1, tiled=True)
    grad_normed = jnp.dot(
        sensitivity_first_factor.astype(jnp.bfloat16),
        first_factor_matrix.T,
        preferred_element_type=jnp.float32,
    )
    grad_normed = grad_normed + jnp.dot(
        grad_right.astype(jnp.bfloat16), second_factor_matrix.T, preferred_element_type=jnp.float32
    )
    gain_applied = grad_normed * standardize_multiplier
    alignment_gradient = averaged_result * (
        gain_applied
        - jnp.mean(gain_applied, axis=-1, keepdims=True)
        - whitened_features * jnp.mean(gain_applied * whitened_features, axis=-1, keepdims=True)
    )
    return (updated_pair_state, alignment_gradient)


def solution(mesh):
    return jax.shard_map(
        local,
        mesh=mesh,
        in_specs=(
            P(None, ("branch", "res"), None),
            P(),
            P(),
            P(),
            P(),
            P(),
            P(),
            P(("branch", "res"), None, None),
            P(("branch", "res"), None, None),
            P(("branch", "res")),
            P(("branch", "res")),
        ),
        out_specs=(P(("branch", "res"), None, None), P(None, ("branch", "res"), None)),
        check_vma=False,
    )
```

profile of v0, /device:TPU:1, one launch (start us, length us, event | category | flops | bytes accessed | tf_op | source)
XLA Modules:
  0.0 905.9 jit_solution(3054021905875174772)
XLA Ops:
  8.3 1.2 fusion.45
  9.5 1.9 convolution_convert_fusion
  12.9 38.6 %all-gather = s32[128,8,2]{1,2,0:T(2,128)S(1)} all-gather(s32[1,8,2]{1,2,0:T(2,128)S(1)} %add_bitcast_fusion), channel_id=1, replica_groups=mesh['branch'=2,'res'=64] {'branch','res'}, dimensions={0}, use_global_device_ids=true | all-gather | bytes 8256 | tf_op jit(solution)/shard_map/all_gather | solution.py:47
  51.7 1.3 convolution_convert_fusion.1
  54.1 62.4 %all-gather.3.cloned.1.call-done = bf16[64,1024,32]{2,1,0:T(8,128)(2,1)} async-done(((bf16[64,8,32]{2,1,0:T(8,128)(2,1)}), bf16[64,1024,32]{2,1,0:T(8,128)(2,1)}) %all-gather.3.cloned.1.call-update) | async-done | bytes 4194320 | tf_op jit(solution)/shard_map/all_gather | solution.py:53
  116.5 16.1 %copy.22 = bf16[64,1024,32]{1,0,2:T(8,128)(2,1)} copy(bf16[64,1024,32]{2,1,0:T(8,128)(2,1)} %all-gather.3.cloned.1.call-done) | data formatting | bytes 8388608 | tf_op jit(solution)/shard_map/while | solution.py:79
  132.6 78.5 %while.12 = (s32[]{:T(128)}, bf16[8,1024,128]{2,1,0:T(8,128)(2,1)}, bf16[8,1024,32,32]{1,3,2,0:T(8,128)(2,1)}, bf16[8,1024,128]{2,1,0:T(8,128)(2,1)}, f32[8,1024...) while((s32[]{:T(128)}, bf16[8,1024,128]{2,1,0:T(8,128)(2,1)}, ...), condition=%wide.region_3.4_spmd, body=%wide.region_2.3_spmd.sunk | while | flops 676200448 | bytes 20223128 | solution.py:79
  132.6 1.7 multiply_convert_fusion.3
  134.3 2.9 fusion.76
  137.2 1.2 copy.44
  138.4 2.6 fusion.77
  140.9 1.5 constant_dynamic-update-slice_fusion.2
  142.4 1.7 multiply_convert_fusion.3
  144.1 2.9 fusion.76
  147.0 1.2 copy.44
  148.2 2.6 fusion.77
  150.8 1.5 constant_dynamic-update-slice_fusion.2
  152.3 1.7 multiply_convert_fusion.3
  154.0 2.9 fusion.76
  156.9 1.2 copy.44
  158.0 2.6 fusion.77
  160.6 1.5 constant_dynamic-update-slice_fusion.2
  162.1 1.7 multiply_convert_fusion.3
  163.8 2.9 fusion.76
  166.7 1.2 copy.44
  167.8 2.6 fusion.77
  170.4 1.5 constant_dynamic-update-slice_fusion.2
  171.9 1.7 multiply_convert_fusion.3
  173.6 2.9 fusion.76
  177.6 2.6 fusion.77
  180.2 1.5 constant_dynamic-update-slice_fusion.2
  181.7 1.7 multiply_convert_fusion.3
  183.4 2.9 fusion.76
  186.3 1.2 copy.44
  187.5 2.6 fusion.77
  190.1 1.5 constant_dynamic-update-slice_fusion.2
  191.5 1.7 multiply_convert_fusion.3
  193.2 2.9 fusion.76
  197.3 2.6 fusion.77
  199.8 1.5 constant_dynamic-update-slice_fusion.2
  201.4 1.7 multiply_convert_fusion.3
  203.0 2.9 fusion.76
  207.1 2.6 fusion.77
  209.7 1.5 constant_dynamic-update-slice_fusion.2
  211.1 25.3 %bitcast_multiply_fusion = f32[64,1024,32]{0,1,2:T(8,128)} fusion(bf16[8,1024,32,32]{1,3,2,0:T(8,128)(2,1)} %get-tuple-element.66, bf16[64,8,32]{0,2,1:T(8,128)(2,1)S(1)} %copy.26), kind=kOutput, calls=%fused_computation.19 | convolution fusion | flops 1075838976 | bytes 25198592 | tf_op jit(solution)/shard_map/fctr,nft->ncr/dot_general | solution.py:91
  236.4 27.4 %copy.23 = bf16[64,1024,32]{0,1,2:T(8,128)(2,1)} copy(bf16[64,1024,32]{2,1,0:T(8,128)(2,1)} %all-gather.3.cloned.1.call-done) | data formatting | bytes 8388608 | tf_op jit(solution)/shard_map/all_gather | solution.py:53
  263.8 26.5 %fusion.31 = bf16[64,8,32]{0,2,1:T(8,128)(2,1)S(1)} fusion(bf16[8,1024,32,32]{1,3,2,0:T(8,128)(2,1)} %get-tuple-element.66, bf16[64,1024,32]{0,1,2:T(8,128)(2,1)} %copy.23), kind=kOutput, calls=%fused_computation.31 | convolution fusion | flops 1073774592 | bytes 21004288 | tf_op jit(solution)/shard_map/prut,ort->opu/dot_general | solution.py:85
  290.7 605.4 %reduce-scatter.2.cloned.1.call-done = f32[64,8,32]{0,1,2:T(8,128)} async-done(((f32[64,1024,32]{0,1,2:T(8,128)}), f32[64,8,32]{0,1,2:T(8,128)}) %reduce-scatter.2.cloned.1.call-update) | async-done | bytes 65552 | tf_op jit(solution)/shard_map/reduce_scatter | solution.py:96
  (50 shorter events, 10.3 us)
Async XLA Ops:
  7.2 2.4 copy-start
  7.2 109.3 %all-gather.3.cloned.1.call-start = ((), (), s32[]{:S(2)}) async-start(), calls=%async_computation.1 | async-start | bytes 16908288 | tf_op jit(solution)/shard_map/all_gather | solution.py:53
  11.5 884.6 %reduce-scatter.2.cloned.1.call-start = ((), (), s32[]{:S(2)}) async-start(), calls=%async_computation.2 | async-start | bytes 16908288 | tf_op jit(solution)/shard_map/reduce_scatter | solution.py:96
  54.1 78.5 %copy-start.1 = (bf16[1024,128]{1,0:T(8,128)(2,1)S(1)}, bf16[1024,128]{1,0:T(8,128)(2,1)}, u32[]{:S(2)}) copy-start(bf16[1024,128]{1,0:T(8,128)(2,1)} %param.17) | copy-start | bytes 786436
  54.1 78.5 %copy-start.5 = (f32[128]{0:T(128)S(1)}, f32[128]{0:T(128)}, u32[]{:S(2)}) copy-start(f32[128]{0:T(128)} %param.18) | copy-start | bytes 1540
  54.1 78.5 %copy-start.6 = (f32[128]{0:T(128)S(1)}, f32[128]{0:T(128)}, u32[]{:S(2)}) copy-start(f32[128]{0:T(128)} %param.19) | copy-start | bytes 1540
  263.8 26.7 %copy-start.3 = (bf16[256,32]{0,1:T(8,128)(2,1)S(1)}, bf16[256,32]{0,1:T(8,128)(2,1)}, u32[]{:S(2)}) copy-start(bf16[256,32]{0,1:T(8,128)(2,1)} %param.15) | copy-start | bytes 49156
  263.8 633.4 %copy-start.2 = (bf16[64,8,256]{2,1,0:T(8,128)(2,1)S(1)}, bf16[64,8,256]{2,1,0:T(8,128)(2,1)}, u32[]{:S(2)}) copy-start(bf16[64,8,256]{2,1,0:T(8,128)(2,1)} %param.13) | copy-start | bytes 786436
  263.8 633.4 %copy-start.4 = (f32[256]{0:T(256)S(1)}, f32[256]{0:T(256)}, u32[]{:S(2)}) copy-start(f32[256]{0:T(256)} %param.14) | copy-start | bytes 3076
Sparse Core Ops, SparseCore 0:
  11.6 104.7 all-gather.2
  236.5 659.5 reduce-scatter.1
where the time goes:
time: 919 us; the launch traced here: 906 us
  waiting for transfers between devices  668 us (73%)
  matrix products  113 us (12%)
  local copies, waits for them, and re-layouts  65.5 us (7%)
  blocking collectives  38.6 us (4%)
  between operations  14.5 us (2%)
    reduce_scatter x1, waiting for transfers between devices, local(): lax.psum_scatter(partial_terms, ('branch', 'res'), scatter_dimension=1, t...  605 us
    all_gather x1, waiting for transfers between devices, local(): right_all = lax.all_gather(right, ('branch', 'res'), axis=1, tiled=True)  62.4 us
    all_gather x1, blocking collectives, local(): lax.all_gather(jnp.stack([padding_indicator, molecule_identity]), ('branc...  38.6 us
    all_gather x1, local copies, waits for them, and re-layouts, local(): right_all = lax.all_gather(right, ('branch', 'res'), axis=1, tiled=True)  27.4 us
    dot_general x1, matrix products, local(): jnp.einsum('prut,ort->opu', reverse_sweep_full, right_all, preferred_elem...  26.5 us
    dot_general x1, matrix products, local(): jnp.einsum('fctr,nft->ncr', reverse_sweep_full, first_factor, preferred_e...  25.3 us
    dot_general x8, matrix products, row_step(): jnp.einsum('sa,sjb->jab', left_row, right_all, preferred_element_type=jnp...  23.2 us
    dot_general x8, matrix products, row_step(): jnp.dot(tensor_product.reshape(total, FACTOR_WIDTH * FACTOR_WIDTH), final...  20.6 us
  transfers between devices with their start and end apart: 2, of which 2 were waited for; matrix products, arithmetic and copies ran while one was open for 6% of the time, Pallas kernels for 0%

commit v1 on v0

v1 whole, which is shorter than its diff:
```python
import jax
import jax.numpy as jnp
from jax import lax
from jax.experimental import pallas as pl
from jax.experimental.pallas import tpu as pltpu
from jax.sharding import PartitionSpec as P

MESH = pl.DeviceIdType.MESH
F32 = jnp.float32
BF16 = jnp.bfloat16

SEQS = 64
FEAT = 256
FACTOR = 32
EDGE = 128
LENGTH = 1024
OWN = 8
HALF = 1024
WIDE = HALF + 128
EPSILON = 1e-05

PARTS = (0, 1, 2)
GATHER_LANES = ((0, 384), (384, 384), (768, 384))
SCATTER_LANES = ((0, 384), (384, 384), (768, 256))


def axes_of(part):
    return (part % 3, (part + 1) % 3, (part + 2) % 3)


def nt(a, b):
    return lax.dot_general(a, b, (((1,), (1,)), ((), ())), preferred_element_type=F32)


def kernel(
    x_ref, gain_ref, w1_ref, w2_ref, wf_ref, off_ref, smo_ref, edge_hbm, cot_hbm, pad_ref, mol_ref,
    out_hbm, grad_ref,
    cot, edge, right, proj, terms, peer_out, peer_in, slab1, sum1, slab2, sum2, slab3,
    gmat, unit_s, rstd_s, wff, wflat, left_s, grad_s, blk_out, blk_in, fin_s, fin_out, fin_in,
    load_sem, store_sem,
    ag_send, ag_recv, fw_send, fw_recv, rs_send, rs_recv, pr_send, pr_recv, misc_send, misc_recv,
):
    branch, res = lax.axis_index("branch"), lax.axis_index("res")
    core = res % 2
    me = (branch * 2 + res // 32, (res // 8) % 4, (res // 2) % 4)

    def device(at, c):
        return (at[0] // 2, (at[0] % 2) * 32 + at[1] * 8 + at[2] * 2 + c)

    def shifted(axis, k):
        at = list(me)
        at[axis] = (at[axis] + k) % 4
        return at

    sibling = device(me, 1 - core)

    barrier = pltpu.get_barrier_semaphore()
    for axis in range(3):
        for k in (1, 2, 3):
            pl.semaphore_signal(barrier, inc=1, device_id=device(shifted(axis, k), core), device_id_type=MESH)
    pl.semaphore_signal(barrier, inc=1, device_id=sibling, device_id_type=MESH)

    cot_loads = [
        pltpu.make_async_copy(cot_hbm.at[i], cot.at[:, pl.ds(i * EDGE, EDGE)], load_sem.at[i])
        for i in range(OWN)
    ]
    for cp in cot_loads:
        cp.start()
    edge_load = pltpu.make_async_copy(edge_hbm, edge, load_sem.at[OWN])
    edge_load.start()

    xs = x_ref[...].astype(F32).reshape(SEQS * OWN, FEAT)
    centred = xs - jnp.mean(xs, axis=-1, keepdims=True)
    rstd = lax.rsqrt(jnp.mean(centred * centred, axis=-1, keepdims=True) + EPSILON)
    unit = centred * rstd
    unit_s[...] = unit
    rstd_s[...] = jnp.broadcast_to(rstd, (SEQS * OWN, 128))
    normed = (unit * gain_ref[...]).astype(BF16)

    lane = lax.broadcasted_iota(jnp.int32, (FACTOR, FEAT), 1)
    row = lax.broadcasted_iota(jnp.int32, (FACTOR, FEAT), 0)
    spread = jnp.where(lane // 8 == row, 1.0, 0.0).astype(BF16)
    w2e = jnp.dot(w2_ref[...], spread, preferred_element_type=F32).astype(BF16)

    rows8 = lax.broadcasted_iota(jnp.int32, (OWN, 128), 0)
    keep_col = jnp.zeros((OWN, 128), F32)
    mol_col = jnp.zeros((OWN, 128), F32)
    for i in range(OWN):
        keep_col = jnp.where(rows8 == i, pad_ref[i].astype(F32), keep_col)
        mol_col = jnp.where(rows8 == i, mol_ref[i].astype(F32), mol_col)
    keep_one = keep_col[:, :1]

    lane4 = lax.broadcasted_iota(jnp.int32, (8, OWN, FEAT), 2) % 8
    slot4 = lax.broadcasted_iota(jnp.int32, (8, OWN, FEAT), 0)
    mine = lane4 == slot4
    right_e = jnp.dot(normed, w2e, preferred_element_type=F32).astype(BF16).astype(F32)
    right_e = right_e.reshape(8, 8, OWN, FEAT)
    flat = [
        jnp.sum(jnp.where(mine, right_e[h], 0.0), axis=0) * keep_one for h in range(8)
    ]
    half0 = jnp.concatenate(flat[:4] + [keep_col], axis=1)
    half1 = jnp.concatenate(flat[4:] + [mol_col], axis=1)
    first = core == 0
    blk_out[...] = jnp.where(first, half1, half0)
    own_blk = jnp.where(first, half0, half1)

    pl.semaphore_wait(barrier, 10)
    blk_copy = pltpu.make_async_remote_copy(
        blk_out, blk_in, misc_send.at[0], misc_recv.at[0], device_id=sibling, device_id_type=MESH
    )
    blk_copy.start()

    left_s[...] = jnp.dot(normed, w1_ref[...], preferred_element_type=F32).astype(BF16).astype(F32)
    wff[...] = wf_ref[...].astype(F32)
    for b in range(FACTOR):
        wflat[:, b * EDGE : (b + 1) * EDGE] = wff[pl.ds(b, FACTOR, stride=FACTOR), :].astype(BF16)
    left = jnp.concatenate(
        [
            left_s[pl.ds(i, SEQS, stride=OWN), :] * (pad_ref[i].astype(F32) * (1.0 / SEQS))
            for i in range(OWN)
        ],
        axis=0,
    ).astype(BF16)

    def gather_ref(half, part, phase, at):
        idx = list(at)
        for axis in axes_of(part)[:phase]:
            idx[axis] = slice(None)
        lo, width = GATHER_LANES[part]
        return right.at[half, idx[0], idx[1], idx[2], :, pl.ds(lo, width)]

    def gather_send(part, phase, k):
        block = gather_ref(core, part, phase, me)
        return pltpu.make_async_remote_copy(
            block, block, ag_send.at[part, phase, k - 1], ag_recv.at[part, phase, k - 1],
            device_id=device(shifted(axes_of(part)[phase], k), core), device_id_type=MESH,
        )

    def gather_recv(part, phase, k):
        block = gather_ref(core, part, phase, shifted(axes_of(part)[phase], 4 - k))
        return pltpu.make_async_remote_copy(
            block, block, ag_send.at[part, phase, k - 1], ag_recv.at[part, phase, k - 1],
            device_id=device(shifted(axes_of(part)[phase], 4 - k), core), device_id_type=MESH,
        )

    def forward(part, k, half):
        block = gather_ref(half, part, 2, shifted(axes_of(part)[2], (4 - k) % 4))
        return pltpu.make_async_remote_copy(
            block, block, fw_send.at[part, k], fw_recv.at[part, k],
            device_id=sibling, device_id_type=MESH,
        )

    def scatter_copy(part, phase, k):
        axes = axes_of(part)
        lo, width = SCATTER_LANES[part]
        lanes = pl.ds(lo, width)
        to = shifted(axes[phase], k)
        there = to[axes[phase]]
        if phase == 0:
            idx = [slice(None)] * 3
            idx[axes[0]] = there
            src = terms.at[idx[0], idx[1], idx[2], :, lanes]
            dst = slab1.at[k - 1, :, :, :, lanes]
        elif phase == 1:
            idx = [slice(None)] * 2
            idx[0 if axes[1] < axes[2] else 1] = there
            src = sum1.at[idx[0], idx[1], :, lanes]
            dst = slab2.at[k - 1, :, :, lanes]
        else:
            src = sum2.at[there, :, lanes]
            dst = slab3.at[k - 1, :, lanes]
        return pltpu.make_async_remote_copy(
            src, dst, rs_send.at[part, phase, k - 1], rs_recv.at[part, phase, k - 1],
            device_id=device(to, core), device_id_type=MESH,
        )

    def scatter_add(part, phase):
        axes = axes_of(part)
        lo, width = SCATTER_LANES[part]
        lanes = pl.ds(lo, width)
        for k in (1, 2, 3):
            scatter_copy(part, phase, k).wait_recv()
        here = me[axes[phase]]
        if phase == 0:
            idx = [slice(None)] * 3
            idx[axes[0]] = here
            total = terms[idx[0], idx[1], idx[2], :, lanes].astype(F32)
            for k in range(3):
                total += slab1[k, :, :, :, lanes].astype(F32)
            sum1[:, :, :, lanes] = total.astype(BF16)
        elif phase == 1:
            idx = [slice(None)] * 2
            idx[0 if axes[1] < axes[2] else 1] = here
            total = sum1[idx[0], idx[1], :, lanes].astype(F32)
            for k in range(3):
                total += slab2[k, :, :, lanes].astype(F32)
            sum2[:, :, lanes] = total.astype(BF16)
        else:
            total = sum2[here, :, lanes].astype(F32)
            for k in range(3):
                total += slab3[k, :, lanes].astype(F32)
            fin_s[:, lanes] = total

    def start_all(make, phase):
        for part in PARTS:
            for k in (1, 2, 3):
                make(part, phase, k).start()

    blk_copy.wait_recv()
    theirs = blk_in[...]
    block16 = jnp.concatenate(
        [jnp.where(first, own_blk, theirs), jnp.where(first, theirs, own_blk)], axis=0
    ).astype(BF16)
    right[core, me[0], me[1], me[2]] = block16
    start_all(gather_send, 0)

    def proj_step(n, carry):
        y = jnp.dot(left, wflat[:, pl.ds(pl.multiple_of(n * 256, 256), 256)], preferred_element_type=F32)
        for i in range(OWN):
            for h in range(8):
                tile = y[i * SEQS + h * 8 : i * SEQS + h * 8 + 8]
                pair = jnp.concatenate([tile[:, :EDGE], tile[:, EDGE:]], axis=0).astype(BF16)
                proj[pl.ds(pl.multiple_of(h * 256 + n * 16, 16), 16), i * EDGE : (i + 1) * EDGE] = pair
        return carry

    lax.fori_loop(0, 16, proj_step, 0)

    for cp in cot_loads:
        cp.wait()

    for part in PARTS:
        for k in (1, 2, 3):
            gather_recv(part, 0, k).wait_recv()
    start_all(gather_send, 1)

    def peer_copy(q):
        return pltpu.make_async_remote_copy(
            peer_out.at[q], peer_in.at[q], pr_send.at[q], pr_recv.at[q],
            device_id=sibling, device_id_type=MESH,
        )

    def half_terms(q, half):
        rows = cot[pl.ds(pl.multiple_of(q * 256, 256), 256), :]
        return nt(rows, proj[pl.ds(pl.multiple_of(half * HALF, HALF), HALF), :])

    def peer_step(q, carry):
        peer_out[q] = half_terms(q, 1 - core).astype(BF16)
        peer_copy(q).start()
        return carry

    lax.fori_loop(0, 4, peer_step, 0)

    for part in PARTS:
        for k in (1, 2, 3):
            gather_recv(part, 1, k).wait_recv()
    start_all(gather_send, 2)
    for part in PARTS:
        forward(part, 0, core).start()

    def own_step(q, carry):
        total = half_terms(q, core)
        peer_copy(q).wait_recv()
        total = total + peer_in[q].astype(F32)
        terms[q] = total.astype(BF16).reshape(4, 4, 16, HALF)
        return carry

    lax.fori_loop(0, 4, own_step, 0)
    start_all(scatter_copy, 0)

    for k in (1, 2, 3):
        for part in PARTS:
            gather_recv(part, 2, k).wait_recv()
            forward(part, k, core).start()
    for k in (0, 1, 2, 3):
        for part in PARTS:
            forward(part, k, 1 - core).wait_recv()

    edge_load.wait()

    def store(q):
        rows = pl.ds(pl.multiple_of(q * 256, 256), 256)
        return pltpu.make_async_copy(edge.at[:, rows, :], out_hbm.at[:, rows, :], store_sem.at[q])

    def pair_step(q, carry):
        r0 = right[0, q, :, :, :, 0:HALF].reshape(256, HALF)
        r1 = right[1, q, :, :, :, 0:HALF].reshape(256, HALF)
        keep_j = right[0, q, :, :, :, HALF:WIDE].reshape(256, 128).astype(F32)
        mol_j = right[1, q, :, :, :, HALF:WIDE].reshape(256, 128).astype(F32)
        u = jnp.dot(r0, proj[:HALF, :], preferred_element_type=F32)
        u += jnp.dot(r1, proj[HALF:, :], preferred_element_type=F32)
        rows = pl.ds(pl.multiple_of(q * 256, 256), 256)
        for i in range(OWN):
            same = jnp.where(mol_j == mol_ref[i].astype(F32), 1.0, 0.0)
            extra = (keep_j * pad_ref[i].astype(F32)) * (off_ref[...] + same * smo_ref[...])
            upd = u[:, i * EDGE : (i + 1) * EDGE] + extra
            edge[i, rows, :] = (edge[i, rows, :].astype(F32) + upd).astype(BF16)
        store(q).start()
        return carry

    lax.fori_loop(0, 2, pair_step, 0)
    for part in PARTS:
        scatter_add(part, 0)
        for k in (1, 2, 3):
            scatter_copy(part, 1, k).start()
    lax.fori_loop(2, 4, pair_step, 0)
    for part in PARTS:
        scatter_add(part, 1)
        for k in (1, 2, 3):
            scatter_copy(part, 2, k).start()

    def left_step(h, carry):
        half = h // 4
        lo = pl.multiple_of((h % 4) * 256, 256)
        r = right[half, :, :, :, :, pl.ds(lo, 256)].reshape(LENGTH, 256)
        g = lax.dot_general(r, cot[...], (((0,), (0,)), ((), ())), preferred_element_type=F32)
        for b in range(FACTOR):
            tile = g[b * 8 : b * 8 + 8]
            for i in range(0, OWN, 2):
                pair = jnp.concatenate(
                    [tile[:, i * EDGE : (i + 1) * EDGE], tile[:, (i + 1) * EDGE : (i + 2) * EDGE]], axis=0
                ).astype(BF16)
                gmat[pl.ds(pl.multiple_of(h * 64 + i * 8, 16), 16), b * EDGE : (b + 1) * EDGE] = pair
        return carry

    lax.fori_loop(0, 8, left_step, 0)

    for part in PARTS:
        scatter_add(part, 2)
    fin = fin_s[...]
    fin_out[...] = jnp.where(first, fin[8:], fin[:8])
    fin_mine = jnp.where(first, fin[:8], fin[8:])
    fin_copy = pltpu.make_async_remote_copy(
        fin_out, fin_in, misc_send.at[1], misc_recv.at[1], device_id=sibling, device_id_type=MESH
    )
    fin_copy.start()

    gl = nt(gmat[...], wflat[...])
    for h in range(8):
        for i in range(OWN):
            tile = gl[h * 64 + i * 8 : h * 64 + i * 8 + 8] * (pad_ref[i].astype(F32) * (1.0 / SEQS))
            grad_s[pl.ds(h * 64 + i, 8, stride=OWN), :] = tile
    grad_normed = nt(grad_s[...].astype(BF16), w1_ref[...])

    fin_copy.wait_recv()
    fin_theirs = fin_in[...]
    lo_half = jnp.where(first, fin_mine, fin_theirs) * keep_one
    hi_half = jnp.where(first, fin_theirs, fin_mine) * keep_one
    spread_rows = []
    for h in range(8):
        src = lo_half if h < 4 else hi_half
        base = src[:, (h % 4) * 256 : (h % 4) * 256 + 256]
        spread_rows.append(jnp.where(mine, base[None], 0.0).reshape(8 * OWN, FEAT))
    gr = jnp.concatenate(spread_rows, axis=0).astype(BF16)
    grad_normed = grad_normed + nt(gr, w2e)

    gained = grad_normed * gain_ref[...]
    unit = unit_s[...]
    rstd = rstd_s[:, :1]
    grad = rstd * (
        gained
        - jnp.mean(gained, axis=-1, keepdims=True)
        - unit * jnp.mean(gained * unit, axis=-1, keepdims=True)
    )
    grad_ref[...] = grad.reshape(SEQS, OWN, FEAT)

    blk_copy.wait_send()
    fin_copy.wait_send()
    for part in PARTS:
        for phase in range(3):
            for k in (1, 2, 3):
                gather_send(part, phase, k).wait_send()
                scatter_copy(part, phase, k).wait_send()
        for k in range(4):
            forward(part, k, core).wait_send()
    for q in range(4):
        peer_copy(q).wait_send()
        store(q).wait()


def local(x, gain, w1, w2, wf, off, smo, edge, cot, pad, mol):
    vmem = pl.BlockSpec(memory_space=pltpu.VMEM)
    smem = pl.BlockSpec(memory_space=pltpu.SMEM)
    hbm = pl.BlockSpec(memory_space=pl.ANY)
    dma = pltpu.SemaphoreType.DMA
    return pl.pallas_call(
        kernel,
        out_shape=(
            jax.ShapeDtypeStruct(edge.shape, BF16),
            jax.ShapeDtypeStruct(x.shape, F32),
        ),
        in_specs=[vmem] * 7 + [hbm, hbm, smem, smem],
        out_specs=(hbm, vmem),
        scratch_shapes=[
            pltpu.VMEM((LENGTH, OWN * EDGE), BF16),
            pltpu.VMEM((OWN, LENGTH, EDGE), BF16),
            pltpu.VMEM((2, 4, 4, 4, 16, WIDE), BF16),
            pltpu.VMEM((2 * HALF, OWN * EDGE), BF16),
            pltpu.VMEM((4, 4, 4, 16, HALF), BF16),
            pltpu.VMEM((4, 256, HALF), BF16),
            pltpu.VMEM((4, 256, HALF), BF16),
            pltpu.VMEM((3, 4, 4, 16, HALF), BF16),
            pltpu.VMEM((4, 4, 16, HALF), BF16),
            pltpu.VMEM((3, 4, 16, HALF), BF16),
            pltpu.VMEM((4, 16, HALF), BF16),
            pltpu.VMEM((3, 16, HALF), BF16),
            pltpu.VMEM((SEQS * OWN, FACTOR * EDGE), BF16),
            pltpu.VMEM((SEQS * OWN, FEAT), F32),
            pltpu.VMEM((SEQS * OWN, 128), F32),
            pltpu.VMEM((FACTOR * FACTOR, EDGE), F32),
            pltpu.VMEM((FACTOR, FACTOR * EDGE), BF16),
            pltpu.VMEM((SEQS * OWN, FACTOR), F32),
            pltpu.VMEM((SEQS * OWN, FACTOR), F32),
            pltpu.VMEM((OWN, WIDE), F32),
            pltpu.VMEM((OWN, WIDE), F32),
            pltpu.VMEM((16, HALF), F32),
            pltpu.VMEM((OWN, HALF), F32),
            pltpu.VMEM((OWN, HALF), F32),
            dma((OWN + 1,)),
            dma((4,)),
            dma((3, 3, 3)),
            dma((3, 3, 3)),
            dma((3, 4)),
            dma((3, 4)),
            dma((3, 3, 3)),
            dma((3, 3, 3)),
            dma((4,)),
            dma((4,)),
            dma((2,)),
            dma((2,)),
        ],
        compiler_params=pltpu.CompilerParams(
            collective_id=0, has_side_effects=True, vmem_limit_bytes=56 * 2**20
        ),
        name="outer_product_mean",
    )(x, gain.reshape(1, FEAT), w1, w2, wf, off.reshape(1, EDGE), smo.reshape(1, EDGE), edge, cot, pad, mol)


def solution(mesh):
    rows = ("branch", "res")
    return jax.shard_map(
        local,
        mesh=mesh,
        in_specs=(
            P(None, rows, None), P(), P(), P(), P(), P(), P(),
            P(rows, None, None), P(rows, None, None), P(rows), P(rows),
        ),
        out_specs=(P(rows, None, None), P(None, rows, None)),
        check_vma=False,
    )
```

time: 919 us -> 60.3 us (0.07); the launches traced: 906 us -> 60.1 us
  waiting for transfers between devices: 668 us -> 0 us
  matrix products: 113 us -> 0 us
  local copies, waits for them, and re-layouts: 65.5 us -> 6.82 us
  Pallas kernels: 0 us -> 52.6 us
  blocking collectives: 38.6 us -> 0 us
  between operations: 14.5 us -> 0.65 us
    reduce_scatter x1 -> x0, waiting for transfers between devices: 605 us -> none  [local(): lax.psum_scatter(partial_terms, ('branch', 'res'), scatter_dimension=1, t...]
    dot_general x30 -> x0, matrix products: 113 us -> none  [the longest x1 26.5 us: local(): jnp.einsum('prut,ort->opu', reverse_sweep_full, right_all, preferred_elem...]
    all_gather x1 -> x0, waiting for transfers between devices: 62.4 us -> none  [local(): right_all = lax.all_gather(right, ('branch', 'res'), axis=1, tiled=True)]
    pallas_call x0 -> x1, Pallas kernels: none -> 52.6 us  [local(): pl.pallas_call(kernel, out_shape=(jax.ShapeDtypeStruct(edge.shape, BF16),...]
    all_gather x1 -> x0, blocking collectives: 38.6 us -> none  [local(): lax.all_gather(jnp.stack([padding_indicator, molecule_identity]), ('branc...]
    all_gather x2 -> x0, local copies, waits for them, and re-layouts: 27.4 us -> none  [the longest x1 27.4 us: local(): right_all = lax.all_gather(right, ('branch', 'res'), axis=1, tiled=True)]
    while x2 -> x0, local copies, waits for them, and re-layouts: 16.3 us -> none  [local(): lax.scan(row_step, jnp.float32(0), (first_factor_sequences, edge_activati...]
    dynamic_update_slice x8 -> x0, local copies, waits for them, and re-layouts: 12 us -> none  [local(): lax.scan(row_step, jnp.float32(0), (first_factor_sequences, edge_activati...]
  transfers between devices with their start and end apart: 2 -> 0, of which waited for: 2 -> 0; matrix products, arithmetic and copies ran while one was open for 6% -> 0% of each run, Pallas kernels for 0% -> 0%
where the time goes in v1:
time: 60.3 us; the launch traced here: 60.1 us
  Pallas kernels  52.6 us (87%)
  local copies, waits for them, and re-layouts  6.82 us (11%)
  between operations  0.65 us (1%)
    pallas_call x1, Pallas kernels, local(): pl.pallas_call(kernel, out_shape=(jax.ShapeDtypeStruct(edge.shape, BF16),...  52.6 us
    unnamed x6, local copies, waits for them, and re-layouts  6.82 us

profile of v1, /device:TPU:1, one launch (start us, length us, event | category | flops | bytes accessed | tf_op | source)
XLA Modules:
  0.0 60.1 jit_solution(8876036184570310437)
XLA Ops:
  0.6 1.5 %copy.13.w1_ref = bf16[256,32]{1,0:T(8,128)(2,1)} copy(bf16[256,32]{0,1:T(8,128)(2,1)} %param.13) | data formatting | bytes 32768 | tf_op args[2]
  2.1 1.4 %copy.14.w2_ref = bf16[256,32]{1,0:T(8,128)(2,1)} copy(bf16[256,32]{0,1:T(8,128)(2,1)} %param.14) | data formatting | bytes 32768 | tf_op args[3]
  3.5 52.6 %outer_product_mean.1 = (bf16[8,1024,128]{2,1,0:T(8,128)(2,1)}, f32[64,8,256]{2,1,0:T(8,128)}) custom-call(bf16[64,8,256]{2,1,0:T(8,128)(2,1)} %x_ref.1, f32[1,256]{1,0:T(1,128)} %bitcast.3, bf16[256,32]{1,0:T(8,128)(2,1)} %copy.13.w1_ref, bf16[256,32]{1,0:T(8,128)(2,1)} %copy.14.w2_ref, bf16[1024,128]{1,0:T(8,128)(2,1)} %wf_ref.1, f32[1,128]{1,0:T(1,128)} %bitcast.4, ...), custom_call_target="tpu_custom_call" | custom-call | tf_op jit(solution)/shard_map/outer_product_mean/pallas_call | solution.py:385
  56.1 0.0 copy-start
  56.2 3.1 %copy.17 = bf16[8,1024,128]{2,1,0:T(8,128)(2,1)} copy(bf16[8,1024,128]{2,1,0:T(8,128)(2,1)} %get-tuple-element.4) | data formatting | bytes 4194304
  59.3 0.0 copy-done
  59.3 0.8 %copy.18 = f32[64,8,256]{2,1,0:T(8,128)} copy(f32[64,8,256]{2,1,0:T(8,128)S(1)} %copy-done) | data formatting | bytes 1048576
Async XLA Ops:
  56.1 3.1 %copy-start = (f32[64,8,256]{2,1,0:T(8,128)S(1)}, f32[64,8,256]{2,1,0:T(8,128)}, u32[]{:S(2)}) copy-start(f32[64,8,256]{2,1,0:T(8,128)} %get-tuple-element.5) | copy-start | bytes 1572868

commit v2 on v0

v2 whole, which is shorter than its diff:
```python
import jax
import jax.numpy as jnp
from jax import lax
from jax.experimental import pallas as pl
from jax.experimental.pallas import tpu as pltpu
from jax.sharding import PartitionSpec as P

MESH = pl.DeviceIdType.MESH
F32 = jnp.float32
BF16 = jnp.bfloat16

SEQS = 64
FEAT = 256
FACTOR = 32
EDGE = 128
LENGTH = 1024
OWN = 8
HALF = 1024
GROUPS = HALF // 128
EPSILON = 1e-05

PARTS = (0, 1, 2)
STEPS = (1, 2, 3)


def axes_of(part):
    return (part % 3, (part + 1) % 3, (part + 2) % 3)


def sum_groups(part):
    return pl.ds(3 * part, 3 if part < 2 else GROUPS - 6)


def nt(a, b):
    return lax.dot_general(a, b, (((1,), (1,)), ((), ())), preferred_element_type=F32)


def normalise(x):
    xs = x.astype(F32).reshape(SEQS * OWN, FEAT)
    centred = xs - jnp.mean(xs, axis=-1, keepdims=True)
    rstd = lax.rsqrt(jnp.mean(centred * centred, axis=-1, keepdims=True) + EPSILON)
    return centred * rstd, rstd


def exchange_kernel(
    x_hbm, gain_hbm, w1t_hbm, w2t_hbm, wf_hbm, edge_hbm, cot_hbm, pad_hbm, mol_hbm,
    u_acc, labels, gn_ref, unit_ref, rstd_ref,
    x_ref, gain_ref, w1t_ref, w2t_ref, wf_ref, pad_ref, mol_ref,
    edge, cot, right, left_b, proj, terms, peer_out, peer_in, slab1, sum1, slab2, sum2, slab3,
    g_acc, gmat, wff, wflat, left_s, grad_s, blk_out, blk_in, fin_s, fin_out, fin_in,
    load_sem,
    ag_send, ag_recv, op_send, op_recv, fw_send, fw_recv,
    r0_send, r0_recv, rs_send, rs_recv, pr_send, pr_recv, misc_send, misc_recv,
):
    branch, res = lax.axis_index("branch"), lax.axis_index("res")
    core = res % 2
    first = core == 0
    me = (branch * 2 + res // 32, (res // 8) % 4, (res // 2) % 4)

    def device(at, c):
        return (at[0] // 2, (at[0] % 2) * 32 + at[1] * 8 + at[2] * 2 + c)

    def shifted(axis, k):
        at = list(me)
        at[axis] = (at[axis] + k) % 4
        return at

    def remote(src, dst, send, recv, to):
        return pltpu.make_async_remote_copy(src, dst, send, recv, device_id=to, device_id_type=MESH)

    sibling = device(me, 1 - core)

    small = (
        (x_hbm, x_ref), (gain_hbm, gain_ref), (w2t_hbm, w2t_ref), (w1t_hbm, w1t_ref),
        (wf_hbm, wf_ref), (pad_hbm, pad_ref), (mol_hbm, mol_ref),
    )
    small_loads = [
        pltpu.make_async_copy(src, dst, load_sem.at[OWN + n]) for n, (src, dst) in enumerate(small)
    ]
    for cp in small_loads:
        cp.start()

    barrier = pltpu.get_barrier_semaphore()
    for axis in range(3):
        for k in STEPS:
            pl.semaphore_signal(barrier, inc=1, device_id=device(shifted(axis, k), core), device_id_type=MESH)
    pl.semaphore_signal(barrier, inc=1, device_id=sibling, device_id_type=MESH)

    cot_loads = [
        pltpu.make_async_copy(cot_hbm.at[i], cot.at[:, :, :, :, pl.ds(i * EDGE, EDGE)], load_sem.at[i])
        for i in range(OWN)
    ]
    edge_load = pltpu.make_async_copy(edge_hbm, edge, load_sem.at[OWN + 7])
    for cp in cot_loads:
        cp.start()
    edge_load.start()

    for cp in small_loads:
        cp.wait()
    unit, rstd = normalise(x_ref[...])
    unit_ref[...] = unit
    rstd_ref[...] = jnp.broadcast_to(rstd, rstd_ref.shape)
    normed = (unit * gain_ref[...]).astype(BF16)

    lane = lax.broadcasted_iota(jnp.int32, (FACTOR, FEAT), 1)
    row = lax.broadcasted_iota(jnp.int32, (FACTOR, FEAT), 0)
    spread = jnp.where(lane // 8 == row, 1.0, 0.0).astype(BF16)
    w2e = lax.dot_general(
        spread, w2t_ref[...], (((0,), (0,)), ((), ())), preferred_element_type=F32
    ).astype(BF16)

    rows8 = lax.broadcasted_iota(jnp.int32, (OWN, 128), 0)
    keep_col = jnp.zeros((OWN, 128), F32)
    mol_col = jnp.zeros((OWN, 128), F32)
    for i in range(OWN):
        keep_col = jnp.where(rows8 == i, pad_ref[i].astype(F32), keep_col)
        mol_col = jnp.where(rows8 == i, mol_ref[i].astype(F32), mol_col)
    keep_one = keep_col[:, :1]

    lane4 = lax.broadcasted_iota(jnp.int32, (8, OWN, FEAT), 2) % 8
    slot4 = lax.broadcasted_iota(jnp.int32, (8, OWN, FEAT), 0)
    mine = lane4 == slot4
    right_e = nt(normed, w2e).astype(BF16).astype(F32).reshape(8, 8, OWN, FEAT)
    flat = [jnp.sum(jnp.where(mine, right_e[h], 0.0), axis=0) * keep_one for h in range(8)]
    half0 = jnp.concatenate(flat[:4] + [keep_col], axis=1)
    half1 = jnp.concatenate(flat[4:] + [mol_col], axis=1)
    blk_out[...] = jnp.where(first, half1, half0)
    own_blk = jnp.where(first, half0, half1)

    left_s[...] = nt(normed, w1t_ref[...]).astype(BF16).astype(F32)
    wff[...] = wf_ref[...].astype(F32)
    for b in range(FACTOR):
        wflat[:, b * EDGE : (b + 1) * EDGE] = wff[pl.ds(b, FACTOR, stride=FACTOR), :].astype(BF16)
    for i in range(OWN):
        rows = left_s[pl.ds(i, SEQS, stride=OWN), :] * (pad_ref[i].astype(F32) * (1.0 / SEQS))
        for half in range(2):
            left_b[half, i * 32 : i * 32 + 32, :] = rows[half * 32 : half * 32 + 32].astype(BF16)

    def proj_half(half):
        left = left_b[half]

        def step(m, carry):
            for v in range(4):
                n = m * 4 + v
                y = jnp.dot(left, wflat[:, pl.ds(pl.multiple_of(n * 256, 256), 256)], preferred_element_type=F32)
                for i in range(OWN):
                    for h in range(4):
                        tile = y[i * 32 + h * 8 : i * 32 + h * 8 + 8]
                        pair = jnp.concatenate([tile[:, :EDGE], tile[:, EDGE:]], axis=0).astype(BF16)
                        top = pl.multiple_of(half * HALF + h * 256 + n * 16, 16)
                        proj[pl.ds(top, 16), i * EDGE : (i + 1) * EDGE] = pair
            return carry

        lax.fori_loop(0, 4, step, 0)

    proj_half(1 - core)
    pl.semaphore_wait(barrier, 10)
    blk_copy = remote(blk_out, blk_in, misc_send.at[0], misc_recv.at[0], sibling)
    blk_copy.start()
    for cp in cot_loads:
        cp.wait()

    def plane_index(part, phase, at):
        idx = list(at)
        for axis in axes_of(part)[:phase]:
            idx[axis] = slice(None)
        return tuple(idx)

    def block_ref(half, part, phase, at):
        return right.at[(half, pl.ds(3 * part, 3)) + plane_index(part, phase, at)]

    def half_ref(half, part, at, upper):
        idx = list(plane_index(part, 2, at))
        idx[axes_of(part)[0]] = pl.ds(2 * upper, 2)
        return right.at[(half, pl.ds(3 * part, 3)) + tuple(idx)]

    def gather(part, phase, k, receive=False):
        axis = axes_of(part)[phase]
        at = shifted(axis, 4 - k) if receive else me
        block = block_ref(core, part, phase, at)
        to = device(shifted(axis, 4 - k if receive else k), core)
        return remote(block, block, ag_send.at[part, phase, k - 1], ag_recv.at[part, phase, k - 1], to)

    def opposite(part, upper, receive=False):
        axis = axes_of(part)[2]
        k = 3 if upper else 1
        at = shifted(axis, 2) if receive else shifted(axis, 4 - k)
        block = half_ref(core, part, at, upper)
        to = device(shifted(axis, 4 - k if receive else k), core)
        return remote(block, block, op_send.at[part, upper], op_recv.at[part, upper], to)

    def forward(part, k, half):
        if k in (2, 4):
            block = half_ref(half, part, shifted(axes_of(part)[2], 2), int(k == 4))
        else:
            block = block_ref(half, part, 2, shifted(axes_of(part)[2], 4 - k))
        return remote(block, block, fw_send.at[part, k], fw_recv.at[part, k], sibling)

    def peer_copy(q):
        return remote(peer_out.at[q], peer_in.at[q], pr_send.at[q], pr_recv.at[q], sibling)

    def half_terms(q, half):
        rows = cot[q].reshape(256, OWN * EDGE)
        return nt(rows, proj[pl.ds(pl.multiple_of(half * HALF, HALF), HALF), :])

    def scatter_first(part, r, k):
        groups = sum_groups(part)
        q = (me[0] + 1 + r) % 4
        if part == 0:
            return remote(
                terms.at[groups, q], slab1.at[r, groups],
                r0_send.at[0, r, 0], r0_recv.at[0, r, 0], device(shifted(0, 1 + r), core),
            )
        to = shifted(part, k)
        if part == 1:
            src = terms.at[groups, q, to[1]]
        else:
            src = terms.at[groups, q, :, to[2]]
        return remote(
            src, slab1.at[k - 1, groups, q],
            r0_send.at[part, r, k - 1], r0_recv.at[part, r, k - 1], device(to, core),
        )

    def peer_half(r):
        q = (me[0] + 1 + r) % 4
        peer_out[q] = half_terms(q, 1 - core).astype(BF16)
        peer_copy(q).start()

    def own_half(r):
        q = (me[0] + 1 + r) % 4
        total = half_terms(q, core)
        peer_copy(q).wait_recv()
        total = (total + peer_in[q].astype(F32)).astype(BF16)
        for g in range(GROUPS):
            terms[g, q] = total[:, g * 128 : (g + 1) * 128].reshape(4, 4, 16, 128)

    def send_terms(r):
        if r < 3:
            scatter_first(0, r, 0).start()
        for part in (1, 2):
            for k in STEPS:
                scatter_first(part, r, k).start()

    peer_half(0)
    blk_copy.wait_recv()
    theirs = blk_in[...]
    block16 = jnp.concatenate(
        [jnp.where(first, own_blk, theirs), jnp.where(first, theirs, own_blk)], axis=0
    ).astype(BF16)
    for g in range(GROUPS + 1):
        right[core, g, me[0], me[1], me[2]] = block16[:, g * 128 : (g + 1) * 128]
    for part in PARTS:
        for k in STEPS:
            gather(part, 0, k).start()

    proj_half(core)
    peer_half(1)
    own_half(0)
    send_terms(0)
    peer_half(2)
    for part in PARTS:
        for k in STEPS:
            gather(part, 0, k, True).wait_recv()
    for part in PARTS:
        for k in STEPS:
            gather(part, 1, k).start()
    own_half(1)
    send_terms(1)
    peer_half(3)
    own_half(2)
    send_terms(2)
    own_half(3)
    send_terms(3)
    edge_load.wait()
    for i in range(OWN):
        u_acc[:, :, :, :, i * EDGE : (i + 1) * EDGE] = edge[i].astype(F32)
    for part in PARTS:
        for k in STEPS:
            gather(part, 1, k, True).wait_recv()
    for part in PARTS:
        for k in (1, 3):
            gather(part, 2, k).start()
    for part in PARTS:
        forward(part, 0, core).start()

    def scatter(part, phase, k):
        axes = axes_of(part)
        groups = sum_groups(part)
        to = shifted(axes[phase], k)
        there = to[axes[phase]]
        if phase == 1:
            idx = [slice(None)] * 2
            idx[0 if axes[1] < axes[2] else 1] = there
            src, dst = sum1.at[groups, idx[0], idx[1]], slab2.at[k - 1, groups]
        else:
            src, dst = sum2.at[groups, there], slab3.at[k - 1, groups]
        return remote(
            src, dst, rs_send.at[part, phase - 1, k - 1], rs_recv.at[part, phase - 1, k - 1], device(to, core)
        )

    def scatter_add(part, phase):
        axes = axes_of(part)
        here = me[axes[phase]]
        first_group, count = 3 * part, 3 if part < 2 else GROUPS - 6
        if phase == 0:
            if part == 0:
                for r in range(3):
                    scatter_first(0, r, 0).wait_recv()
            else:
                for r in range(4):
                    for k in STEPS:
                        scatter_first(part, r, k).wait_recv()
        else:
            for k in STEPS:
                scatter(part, phase, k).wait_recv()
        for g in range(first_group, first_group + count):
            if phase == 0:
                idx = [slice(None)] * 3
                idx[axes[0]] = here
                total = terms[g, idx[0], idx[1], idx[2]].astype(F32)
                for k in range(3):
                    total += slab1[k, g].astype(F32)
                sum1[g] = total.astype(BF16)
            elif phase == 1:
                idx = [slice(None)] * 2
                idx[0 if axes[1] < axes[2] else 1] = here
                total = sum1[g, idx[0], idx[1]].astype(F32)
                for k in range(3):
                    total += slab2[k, g].astype(F32)
                sum2[g] = total.astype(BF16)
            else:
                total = sum2[g, here].astype(F32)
                for k in range(3):
                    total += slab3[k, g].astype(F32)
                fin_s[:, g * 128 : (g + 1) * 128] = total
        if phase < 2:
            for k in STEPS:
                scatter(part, phase + 1, k).start()

    def flat_plane(ref, lead, part, k):
        idx = plane_index(part, 2, shifted(axes_of(part)[2], (4 - k) % 4))
        return ref[lead + idx].reshape(256, ref.shape[-1])

    def count_of(part):
        return 3 if part < 2 else GROUPS - 6

    def left_plane(half, part, k):
        count = count_of(part)
        block = jnp.concatenate(
            [flat_plane(right, (half, 3 * part + n), part, k) for n in range(count)], axis=1
        )
        prod = lax.dot_general(
            block, flat_plane(cot, (), part, k), (((0,), (0,)), ((), ())), preferred_element_type=F32
        )
        rows = pl.ds(pl.multiple_of(half * HALF + part * 384, 128), count * 128)
        if k == 0:
            g_acc[rows, :] = prod
            return
        prod = prod + g_acc[rows, :]
        if k != 2:
            g_acc[rows, :] = prod
            return
        for n in range(count):
            gi = 3 * part + n
            for b in range(16):
                tile = prod[n * 128 + b * 8 : n * 128 + b * 8 + 8]
                lo = ((gi % 2) * 16 + b) * EDGE
                for m in range(OWN // 2):
                    pair = jnp.concatenate(
                        [tile[:, m * 256 : m * 256 + EDGE], tile[:, m * 256 + EDGE : m * 256 + 256]], axis=0
                    ).astype(BF16)
                    top = pl.multiple_of((half * 4 + gi // 2) * 64 + m * 16, 16)
                    gmat[pl.ds(top, 16), lo : lo + EDGE] = pair

    def pair_plane(part, k):
        count = count_of(part)
        lhs = jnp.concatenate(
            [flat_plane(right, (half, 3 * part + n), part, k) for half in range(2) for n in range(count)], axis=1
        )
        rhs = jnp.concatenate(
            [proj[half * HALF + part * 384 : half * HALF + part * 384 + count * 128, :] for half in range(2)], axis=0
        )
        u = jnp.dot(lhs, rhs, preferred_element_type=F32)
        idx = plane_index(part, 2, shifted(axes_of(part)[2], (4 - k) % 4))
        u_acc[idx] = u_acc[idx] + u.reshape(4, 4, 16, OWN * EDGE)

    def forwarded(k):
        for part in PARTS:
            forward(part, k, 1 - core).wait_recv()
            if k == 2:
                forward(part, 4, 1 - core).wait_recv()

    def left_own(k):
        for part in PARTS:
            left_plane(core, part, k)

    def left_other(k):
        for part in PARTS:
            left_plane(1 - core, part, k)

    def pair(k):
        for part in PARTS:
            pair_plane(part, k)

    def neighbours():
        for k in (1, 3):
            for part in PARTS:
                gather(part, 2, k, True).wait_recv()
                opposite(part, int(k == 3)).start()
                forward(part, k, core).start()

    def opposites():
        for part in PARTS:
            for upper in (0, 1):
                opposite(part, upper, True).wait_recv()
                forward(part, 2 + 2 * upper, core).start()

    def reduce(phase):
        for part in PARTS:
            scatter_add(part, phase)

    def left_gradient():
        gl = nt(gmat[...], wflat[...])
        for h in range(8):
            for i in range(OWN):
                tile = gl[h * 64 + i * 8 : h * 64 + i * 8 + 8] * (pad_ref[i].astype(F32) * (1.0 / SEQS))
                grad_s[pl.ds(h * 64 + i, 8, stride=OWN), :] = tile
        gn_ref[...] = jnp.dot(grad_s[...].astype(BF16), w1t_ref[...], preferred_element_type=F32)

    left_own(0)
    forwarded(0)
    left_other(0)
    pair(0)
    neighbours()
    left_own(1)
    left_own(3)
    reduce(0)
    forwarded(1)
    left_other(1)
    forwarded(3)
    left_other(3)
    opposites()
    pair(1)
    left_own(2)
    reduce(1)
    pair(3)
    forwarded(2)
    left_other(2)
    pair(2)
    for half in range(2):
        labels[half] = right[half, GROUPS]
    reduce(2)
    fin = fin_s[...]
    fin_out[...] = jnp.where(first, fin[8:], fin[:8])
    fin_mine = jnp.where(first, fin[:8], fin[8:])
    fin_copy = remote(fin_out, fin_in, misc_send.at[1], misc_recv.at[1], sibling)
    fin_copy.start()
    left_gradient()

    fin_copy.wait_recv()
    fin_theirs = fin_in[...]
    lo_half = jnp.where(first, fin_mine, fin_theirs) * keep_one
    hi_half = jnp.where(first, fin_theirs, fin_mine) * keep_one
    spread_rows = []
    for h in range(8):
        src = lo_half if h < 4 else hi_half
        base = src[:, (h % 4) * 256 : (h % 4) * 256 + 256]
        spread_rows.append(jnp.where(mine, base[None], 0.0).reshape(8 * OWN, FEAT))
    gr = jnp.concatenate(spread_rows, axis=0).astype(BF16)
    gn_ref[...] += jnp.dot(gr, w2e, preferred_element_type=F32)

    blk_copy.wait_send()
    fin_copy.wait_send()
    for part in PARTS:
        for k in STEPS:
            for phase in (1, 2):
                scatter(part, phase, k).wait_send()
            gather(part, 0, k).wait_send()
            gather(part, 1, k).wait_send()
        for k in (1, 3):
            gather(part, 2, k).wait_send()
        for upper in (0, 1):
            opposite(part, upper).wait_send()
        for k in range(5):
            forward(part, k, core).wait_send()
    for r in range(4):
        if r < 3:
            scatter_first(0, r, 0).wait_send()
        for part in (1, 2):
            for k in STEPS:
                scatter_first(part, r, k).wait_send()
        peer_copy(r).wait_send()


def finish_kernel(
    u_ref, labels, gn_ref, unit_ref, rstd_ref, gain_ref, off_ref, smo_ref, pad_ref, mol_ref,
    pair_out, grad_out, held, grad, sems,
):
    stores = [pltpu.make_async_copy(held.at[i], pair_out.at[i], sems.at[i]) for i in range(OWN)]
    grad_store = pltpu.make_async_copy(grad, grad_out, sems.at[OWN])
    keep_j = labels[0].astype(F32)
    mol_j = labels[1].astype(F32)
    apart = keep_j * off_ref[...]
    together = keep_j * (off_ref[...] + smo_ref[...])

    def pair(i):
        extra = jnp.where(mol_j == mol_ref[i].astype(F32), together, apart) * pad_ref[i].astype(F32)
        held[i] = (u_ref[:, i * EDGE : (i + 1) * EDGE] + extra).astype(BF16)
        stores[i].start()

    for i in range(4):
        pair(i)
    unit = unit_ref[...]
    gained = gn_ref[...] * gain_ref[...]
    result = rstd_ref[:, :1] * (
        gained
        - jnp.mean(gained, axis=-1, keepdims=True)
        - unit * jnp.mean(gained * unit, axis=-1, keepdims=True)
    )
    grad[...] = result.reshape(SEQS, OWN, FEAT)
    grad_store.start()
    for i in range(4, OWN):
        pair(i)
    for cp in stores:
        cp.wait()
    grad_store.wait()


def local(x, gain, w1, w2, wf, off, smo, edge, cot, pad, mol):
    vmem = pl.BlockSpec(memory_space=pltpu.VMEM)
    smem = pl.BlockSpec(memory_space=pltpu.SMEM)
    hbm = pl.BlockSpec(memory_space=pl.ANY)
    dma = pltpu.SemaphoreType.DMA
    gain = gain.reshape(1, FEAT)
    operands = (x, gain, w1.T, w2.T, wf) + tuple(
        v.reshape(OWN, 4, 4, 4, 16, EDGE) for v in (edge, cot)
    ) + (pad, mol)
    u, labels, gn, unit, rstd = pl.pallas_call(
        exchange_kernel,
        out_shape=(
            pltpu.VMEM((4, 4, 4, 16, OWN * EDGE), F32),
            pltpu.VMEM((2, 4, 4, 4, 16, 128), BF16),
            pltpu.VMEM((SEQS * OWN, FEAT), F32),
            pltpu.VMEM((SEQS * OWN, FEAT), F32),
            pltpu.VMEM((SEQS * OWN, 128), F32),
        ),
        in_specs=[hbm] * 9,
        out_specs=(vmem,) * 5,
        scratch_shapes=[
            pltpu.VMEM((SEQS, OWN, FEAT), BF16),
            pltpu.VMEM((1, FEAT), F32),
            pltpu.VMEM((FACTOR, FEAT), BF16),
            pltpu.VMEM((FACTOR, FEAT), BF16),
            pltpu.VMEM((FACTOR * FACTOR, EDGE), BF16),
            pltpu.SMEM((OWN,), jnp.int32),
            pltpu.SMEM((OWN,), jnp.int32),
            pltpu.VMEM((OWN, 4, 4, 4, 16, EDGE), BF16),
            pltpu.VMEM((4, 4, 4, 16, OWN * EDGE), BF16),
            pltpu.VMEM((2, GROUPS + 1, 4, 4, 4, 16, 128), BF16),
            pltpu.VMEM((2, OWN * 32, FACTOR), BF16),
            pltpu.VMEM((2 * HALF, OWN * EDGE), BF16),
            pltpu.VMEM((GROUPS, 4, 4, 4, 16, 128), BF16),
            pltpu.VMEM((4, 256, HALF), BF16),
            pltpu.VMEM((4, 256, HALF), BF16),
            pltpu.VMEM((3, GROUPS, 4, 4, 16, 128), BF16),
            pltpu.VMEM((GROUPS, 4, 4, 16, 128), BF16),
            pltpu.VMEM((3, GROUPS, 4, 16, 128), BF16),
            pltpu.VMEM((GROUPS, 4, 16, 128), BF16),
            pltpu.VMEM((3, GROUPS, 16, 128), BF16),
            pltpu.VMEM((2 * HALF, OWN * EDGE), F32),
            pltpu.VMEM((SEQS * OWN, FACTOR * EDGE), BF16),
            pltpu.VMEM((FACTOR * FACTOR, EDGE), F32),
            pltpu.VMEM((FACTOR, FACTOR * EDGE), BF16),
            pltpu.VMEM((SEQS * OWN, FACTOR), F32),
            pltpu.VMEM((SEQS * OWN, FACTOR), F32),
            pltpu.VMEM((OWN, HALF + 128), F32),
            pltpu.VMEM((OWN, HALF + 128), F32),
            pltpu.VMEM((16, HALF), F32),
            pltpu.VMEM((OWN, HALF), F32),
            pltpu.VMEM((OWN, HALF), F32),
            dma((OWN + 8,)),
            dma((3, 3, 3)),
            dma((3, 3, 3)),
            dma((3, 2)),
            dma((3, 2)),
            dma((3, 5)),
            dma((3, 5)),
            dma((3, 4, 3)),
            dma((3, 4, 3)),
            dma((3, 2, 3)),
            dma((3, 2, 3)),
            dma((4,)),
            dma((4,)),
            dma((2,)),
            dma((2,)),
        ],
        compiler_params=pltpu.CompilerParams(
            collective_id=0, has_side_effects=True, vmem_limit_bytes=50 * 2**20
        ),
        name="outer_product_mean",
    )(*(pltpu.with_memory_space_constraint(v, pltpu.HBM) for v in operands))
    return pl.pallas_call(
        finish_kernel,
        out_shape=(
            jax.ShapeDtypeStruct(edge.shape, BF16),
            jax.ShapeDtypeStruct(x.shape, F32),
        ),
        in_specs=[vmem] * 8 + [smem, smem],
        out_specs=(hbm, hbm),
        scratch_shapes=[
            pltpu.VMEM((OWN, LENGTH, EDGE), BF16),
            pltpu.VMEM((SEQS, OWN, FEAT), F32),
            dma((OWN + 1,)),
        ],
        compiler_params=pltpu.CompilerParams(vmem_limit_bytes=16 * 2**20),
        name="finish",
    )(
        u.reshape(LENGTH, OWN * EDGE), labels.reshape(2, LENGTH, 128), gn, unit, rstd, gain,
        off.reshape(1, EDGE), smo.reshape(1, EDGE), pad, mol,
    )


def solution(mesh):
    rows = ("branch", "res")
    return jax.shard_map(
        local,
        mesh=mesh,
        in_specs=(
            P(None, rows, None), P(), P(), P(), P(), P(), P(),
            P(rows, None, None), P(rows, None, None), P(rows), P(rows),
        ),
        out_specs=(P(rows, None, None), P(None, rows, None)),
        check_vma=False,
    )
```

time: 919 us -> 49.9 us (0.05); the launches traced: 906 us -> 49.8 us
  waiting for transfers between devices: 668 us -> 0 us
  matrix products: 113 us -> 0 us
  local copies, waits for them, and re-layouts: 65.5 us -> 0.02 us
  Pallas kernels: 0 us -> 48.9 us
  blocking collectives: 38.6 us -> 0 us
  between operations: 14.5 us -> 0.88 us
    reduce_scatter x1 -> x0, waiting for transfers between devices: 605 us -> none  [local(): lax.psum_scatter(partial_terms, ('branch', 'res'), scatter_dimension=1, t...]
    dot_general x30 -> x0, matrix products: 113 us -> none  [the longest x1 26.5 us: local(): jnp.einsum('prut,ort->opu', reverse_sweep_full, right_all, preferred_elem...]
    all_gather x1 -> x0, waiting for transfers between devices: 62.4 us -> none  [local(): right_all = lax.all_gather(right, ('branch', 'res'), axis=1, tiled=True)]
    pallas_call x0 -> x2, Pallas kernels: none -> 48.9 us  [the longest x1 45.3 us: local(): pl.pallas_call(exchange_kernel, out_shape=(pltpu.VMEM((4, 4, 4, 16, OWN *...]
    all_gather x1 -> x0, blocking collectives: 38.6 us -> none  [local(): lax.all_gather(jnp.stack([padding_indicator, molecule_identity]), ('branc...]
    all_gather x2 -> x0, local copies, waits for them, and re-layouts: 27.4 us -> none  [the longest x1 27.4 us: local(): right_all = lax.all_gather(right, ('branch', 'res'), axis=1, tiled=True)]
    while x2 -> x0, local copies, waits for them, and re-layouts: 16.3 us -> none  [local(): lax.scan(row_step, jnp.float32(0), (first_factor_sequences, edge_activati...]
    dynamic_update_slice x8 -> x0, local copies, waits for them, and re-layouts: 12 us -> none  [local(): lax.scan(row_step, jnp.float32(0), (first_factor_sequences, edge_activati...]
  transfers between devices with their start and end apart: 2 -> 0, of which waited for: 2 -> 0; matrix products, arithmetic and copies ran while one was open for 6% -> 0% of each run, Pallas kernels for 0% -> 0%
where the time goes in v2:
time: 49.9 us; the launch traced here: 49.8 us
  Pallas kernels  48.9 us (98%)
  between operations  0.88 us (2%)
    pallas_call x1, Pallas kernels, local(): pl.pallas_call(exchange_kernel, out_shape=(pltpu.VMEM((4, 4, 4, 16, OWN *...  45.3 us
    pallas_call x1, Pallas kernels, local(): pl.pallas_call(finish_kernel, out_shape=(jax.ShapeDtypeStruct(edge.shape,...  3.55 us

profile of v2, /device:TPU:1, one launch (start us, length us, event | category | flops | bytes accessed | tf_op | source)
XLA Modules:
  0.0 49.8 jit_solution(13244340249189242125)
XLA Ops:
  0.6 0.0 copy-start
  0.6 0.0 copy-start.1
  0.7 0.0 copy-start.2
  0.7 0.0 copy-start.3
  0.7 0.0 copy-start.4
  0.7 45.3 %outer_product_mean.1 = (f32[4,4,4,16,1024]{4,3,2,1,0:T(8,128)S(1)}, bf16[2,4,4,4,16,128]{5,4,3,2,1,0:T(8,128)(2,1)S(1)}, f32[512,256]{1,0:T(8,128)S(1)}, f32[512,256]{1,0:T(8,128)S(1)}, f32[512,128]{1,0:T(8,128)S(1)}) custom-call(bf16[64,8,256]{2,1,0:T(8,128)(2,1)} %x_hbm.1, f32[1,256]{1,0:T(1,128)} %bitcast.11, bf16[32,256]{1,0:T(8,128)(2,1)} %bitcast.17, ...), custom_call_target="tpu_custom_call" | custom-call | tf_op jit(solution)/shard_map/outer_product_mean/pallas_call | solution.py:538
  46.0 0.0 copy-done
  46.0 0.0 copy-done.1
  46.0 0.0 copy-done.2
  46.0 0.0 copy-done.3
  46.1 0.0 copy-done.4
  46.1 3.6 %finish.1 = (bf16[8,1024,128]{2,1,0:T(8,128)(2,1)}, f32[64,8,256]{2,1,0:T(8,128)}) custom-call(f32[1024,1024]{1,0:T(8,128)S(1)} %bitcast.9, bf16[2,1024,128]{2,1,0:T(8,128)(2,1)S(1)} %bitcast.10, f32[512,256]{1,0:T(8,128)S(1)} %get-tuple-element.9.gn_ref, f32[512,256]{1,0:T(8,128)S(1)} %get-tuple-element.10.unit_ref, ...), custom_call_target="tpu_custom_call" | custom-call | tf_op jit(solution)/shard_map/finish/pallas_call | solution.py:602
Async XLA Ops:
  0.6 45.4 %copy-start = (f32[256]{0:T(256)S(1)}, f32[256]{0:T(256)}, u32[]{:S(2)}) copy-start(f32[256]{0:T(256)} %param.12) | copy-start | bytes 3076
  0.6 45.4 %copy-start.1 = (s32[8]{0:T(128)S(1)}, s32[8]{0:T(128)}, u32[]{:S(2)}) copy-start(s32[8]{0:T(128)} %pad_ref.1) | copy-start | bytes 100
  0.7 45.4 %copy-start.2 = (s32[8]{0:T(128)S(1)}, s32[8]{0:T(128)}, u32[]{:S(2)}) copy-start(s32[8]{0:T(128)} %mol_ref.1) | copy-start | bytes 100
  0.7 45.4 %copy-start.3 = (f32[128]{0:T(128)S(1)}, f32[128]{0:T(128)}, u32[]{:S(2)}) copy-start(f32[128]{0:T(128)} %param.16) | copy-start | bytes 1540
  0.7 45.4 %copy-start.4 = (f32[128]{0:T(128)S(1)}, f32[128]{0:T(128)}, u32[]{:S(2)}) copy-start(f32[128]{0:T(128)} %param.17) | copy-start | bytes 1540

commit v3 on v2

--- a/solution.py
+++ b/solution.py
@@ -21,6 +21,8 @@
 
 PARTS = (0, 1, 2)
 STEPS = (1, 2, 3)
+FORWARD = (0, 1, 3, 2, 3)
+PLANE = tuple((k, m) for k in range(4) for m in range(4) if k or m)
 
 
 def axes_of(part):
@@ -46,10 +48,10 @@
     x_hbm, gain_hbm, w1t_hbm, w2t_hbm, wf_hbm, edge_hbm, cot_hbm, pad_hbm, mol_hbm,
     u_acc, labels, gn_ref, unit_ref, rstd_ref,
     x_ref, gain_ref, w1t_ref, w2t_ref, wf_ref, pad_ref, mol_ref,
-    edge, cot, right, left_b, proj, terms, peer_out, peer_in, slab1, sum1, slab2, sum2, slab3,
+    edge, cot, right, left_b, proj, terms, peer_out, peer_in, hop0, hop, slab1, sum1, slab2, sum2, slab3,
     g_acc, gmat, wff, wflat, left_s, grad_s, blk_out, blk_in, fin_s, fin_out, fin_in,
     load_sem,
-    ag_send, ag_recv, op_send, op_recv, fw_send, fw_recv,
+    ag_send, ag_recv, nb_send, nb_recv, op_send, op_recv, fw_send, fw_recv,
     r0_send, r0_recv, rs_send, rs_recv, pr_send, pr_recv, misc_send, misc_recv,
 ):
     branch, res = lax.axis_index("branch"), lax.axis_index("res")
@@ -60,37 +62,46 @@
     def device(at, c):
         return (at[0] // 2, (at[0] % 2) * 32 + at[1] * 8 + at[2] * 2 + c)
 
-    def shifted(axis, k):
+    def shifted(axis, k, other=None, m=0):
         at = list(me)
         at[axis] = (at[axis] + k) % 4
+        if other is not None:
+            at[other] = (at[other] + m) % 4
         return at
 
     def remote(src, dst, send, recv, to):
         return pltpu.make_async_remote_copy(src, dst, send, recv, device_id=to, device_id_type=MESH)
 
     sibling = device(me, 1 - core)
+
+    def settle(send, recv, groups, rows, cols):
+        block = right.at[0, pl.ds(0, groups), pl.ds(0, rows), pl.ds(0, cols), 0]
+        return remote(block, block, send, recv, sibling)
 
     small = (
         (x_hbm, x_ref), (gain_hbm, gain_ref), (w2t_hbm, w2t_ref), (w1t_hbm, w1t_ref),
         (wf_hbm, wf_ref), (pad_hbm, pad_ref), (mol_hbm, mol_ref),
     )
     small_loads = [
-        pltpu.make_async_copy(src, dst, load_sem.at[OWN + n]) for n, (src, dst) in enumerate(small)
+        pltpu.make_async_copy(src, dst, load_sem.at[2 + n]) for n, (src, dst) in enumerate(small)
     ]
     for cp in small_loads:
         cp.start()
 
     barrier = pltpu.get_barrier_semaphore()
-    for axis in range(3):
+    for part in PARTS:
+        axes = axes_of(part)
         for k in STEPS:
-            pl.semaphore_signal(barrier, inc=1, device_id=device(shifted(axis, k), core), device_id_type=MESH)
+            for m in range(4):
+                to = device(shifted(axes[0], k, axes[1], m), core)
+                pl.semaphore_signal(barrier, inc=1, device_id=to, device_id_type=MESH)
     pl.semaphore_signal(barrier, inc=1, device_id=sibling, device_id_type=MESH)
 
     cot_loads = [
-        pltpu.make_async_copy(cot_hbm.at[i], cot.at[:, :, :, :, pl.ds(i * EDGE, EDGE)], load_sem.at[i])
+        pltpu.make_async_copy(cot_hbm.at[i], cot.at[:, :, :, :, pl.ds(i * EDGE, EDGE)], load_sem.at[0])
         for i in range(OWN)
     ]
-    edge_load = pltpu.make_async_copy(edge_hbm, edge, load_sem.at[OWN + 7])
+    edge_load = pltpu.make_async_copy(edge_hbm, edge, load_sem.at[1])
     for cp in cot_loads:
         cp.start()
     edge_load.start()
@@ -126,6 +137,10 @@
     half1 = jnp.concatenate(flat[4:] + [mol_col], axis=1)
     blk_out[...] = jnp.where(first, half1, half0)
     own_blk = jnp.where(first, half0, half1)
+
+    pl.semaphore_wait(barrier, 37)
+    blk_copy = remote(blk_out, blk_in, misc_send.at[0], misc_recv.at[0], sibling)
+    blk_copy.start()
 
     left_s[...] = nt(normed, w1t_ref[...]).astype(BF16).astype(F32)
     wff[...] = wf_ref[...].astype(F32)
@@ -153,13 +168,6 @@
 
         lax.fori_loop(0, 4, step, 0)
 
-    proj_half(1 - core)
-    pl.semaphore_wait(barrier, 10)
-    blk_copy = remote(blk_out, blk_in, misc_send.at[0], misc_recv.at[0], sibling)
-    blk_copy.start()
-    for cp in cot_loads:
-        cp.wait()
-
     def plane_index(part, phase, at):
         idx = list(at)
         for axis in axes_of(part)[:phase]:
@@ -174,12 +182,19 @@
         idx[axes_of(part)[0]] = pl.ds(2 * upper, 2)
         return right.at[(half, pl.ds(3 * part, 3)) + tuple(idx)]
 
-    def gather(part, phase, k, receive=False):
-        axis = axes_of(part)[phase]
+    def scattered(part, k, m, receive=False):
+        axes = axes_of(part)
+        there = shifted(axes[0], (4 - k) % 4, axes[1], (4 - m) % 4)
+        block = block_ref(core, part, 0, there if receive else me)
+        to = device(there if receive else shifted(axes[0], k, axes[1], m), core)
+        return remote(block, block, ag_send.at[part], ag_recv.at[part], to)
+
+    def neighbour(part, k, receive=False):
+        axis = axes_of(part)[2]
         at = shifted(axis, 4 - k) if receive else me
-        block = block_ref(core, part, phase, at)
+        block = block_ref(core, part, 2, at)
         to = device(shifted(axis, 4 - k if receive else k), core)
-        return remote(block, block, ag_send.at[part, phase, k - 1], ag_recv.at[part, phase, k - 1], to)
+        return remote(block, block, nb_send.at[part], nb_recv.at[part], to)
 
     def opposite(part, upper, receive=False):
         axis = axes_of(part)[2]
@@ -187,14 +202,14 @@
         at = shifted(axis, 2) if receive else shifted(axis, 4 - k)
         block = half_ref(core, part, at, upper)
         to = device(shifted(axis, 4 - k if receive else k), core)
-        return remote(block, block, op_send.at[part, upper], op_recv.at[part, upper], to)
+        return remote(block, block, op_send.at[part], op_recv.at[part], to)
 
     def forward(part, k, half):
         if k in (2, 4):
             block = half_ref(half, part, shifted(axes_of(part)[2], 2), int(k == 4))
         else:
             block = block_ref(half, part, 2, shifted(axes_of(part)[2], 4 - k))
-        return remote(block, block, fw_send.at[part, k], fw_recv.at[part, k], sibling)
+        return remote(block, block, fw_send.at[FORWARD[k]], fw_recv.at[FORWARD[k]], sibling)
 
     def peer_copy(q):
         return remote(peer_out.at[q], peer_in.at[q], pr_send.at[q], pr_recv.at[q], sibling)
@@ -203,31 +218,56 @@
         rows = cot[q].reshape(256, OWN * EDGE)
         return nt(rows, proj[pl.ds(pl.multiple_of(half * HALF, HALF), HALF), :])
 
-    def scatter_first(part, r, k):
-        groups = sum_groups(part)
-        q = (me[0] + 1 + r) % 4
-        if part == 0:
-            return remote(
-                terms.at[groups, q], slab1.at[r, groups],
-                r0_send.at[0, r, 0], r0_recv.at[0, r, 0], device(shifted(0, 1 + r), core),
-            )
-        to = shifted(part, k)
+    def quarter(r):
+        return (me[0] + (2, 1, 3, 0)[r]) % 4
+
+    def hop_first(upper):
+        groups = sum_groups(0)
+        return remote(
+            terms.at[groups, quarter(0), pl.ds(2 * upper, 2)], hop0.at[upper, groups],
+            r0_send.at[upper], r0_recv.at[upper], device(shifted(0, 3 if upper else 1), core),
+        )
+
+    def slab_first(r):
+        groups = sum_groups(0)
+        return remote(
+            terms.at[groups, quarter(r)], slab1.at[r - 1, groups],
+            r0_send.at[2], r0_recv.at[2], device(shifted(0, 1 if r == 1 else 3), core),
+        )
+
+    def scatter_first(part, r, what):
+        groups, q = sum_groups(part), quarter(r)
+        up = r % 2 == 0 if what == 0 else what == 1
+        there = shifted(part, 2 if what == 0 else (1 if up else 3))
         if part == 1:
-            src = terms.at[groups, q, to[1]]
+            src = terms.at[groups, q, there[1]]
         else:
-            src = terms.at[groups, q, :, to[2]]
+            src = terms.at[groups, q, :, there[2]]
+        dst = hop.at[part - 1, q, groups] if what == 0 else slab1.at[what - 1, groups, q]
+        sem = 3 + r if what == 0 else 6 + part
         return remote(
-            src, slab1.at[k - 1, groups, q],
-            r0_send.at[part, r, k - 1], r0_recv.at[part, r, k - 1], device(to, core),
-        )
+            src, dst, r0_send.at[sem], r0_recv.at[sem],
+            device(shifted(part, 1 if up else 3), core),
+        )
+
+    def combine(r):
+        q = quarter(r)
+        what = 1 if r % 2 == 0 else 2
+        settle(r0_send.at[3 + r], r0_recv.at[3 + r], 5, 4, 1).wait_recv()
+        for part in (1, 2):
+            there = shifted(part, 1 if what == 1 else 3)
+            for g in range(3 * part, 3 * part + (3 if part < 2 else GROUPS - 6)):
+                idx = (g, q, there[1]) if part == 1 else (g, q, slice(None), there[2])
+                terms[idx] = (terms[idx].astype(F32) + hop[part - 1, q, g].astype(F32)).astype(BF16)
+            scatter_first(part, r, what).start()
 
     def peer_half(r):
-        q = (me[0] + 1 + r) % 4
+        q = quarter(r)
         peer_out[q] = half_terms(q, 1 - core).astype(BF16)
         peer_copy(q).start()
 
     def own_half(r):
-        q = (me[0] + 1 + r) % 4
+        q = quarter(r)
         total = half_terms(q, core)
         peer_copy(q).wait_recv()
         total = (total + peer_in[q].astype(F32)).astype(BF16)
@@ -235,13 +275,21 @@
             terms[g, q] = total[:, g * 128 : (g + 1) * 128].reshape(4, 4, 16, 128)
 
     def send_terms(r):
-        if r < 3:
-            scatter_first(0, r, 0).start()
+        if r == 0:
+            for upper in (0, 1):
+                hop_first(upper).start()
         for part in (1, 2):
-            for k in STEPS:
-                scatter_first(part, r, k).start()
-
-    peer_half(0)
+            scatter_first(part, r, 0).start()
+            scatter_first(part, r, 2 if r % 2 == 0 else 1).start()
+
+    def combine_first(r):
+        upper = r - 1
+        hop_first(upper).wait_recv()
+        for g in range(3):
+            idx = (g, quarter(r), pl.ds(2 * upper, 2))
+            terms[idx] = (terms[idx].astype(F32) + hop0[upper, g].astype(F32)).astype(BF16)
+        slab_first(r).start()
+
     blk_copy.wait_recv()
     theirs = blk_in[...]
     block16 = jnp.concatenate(
@@ -249,39 +297,37 @@
     ).astype(BF16)
     for g in range(GROUPS + 1):
         right[core, g, me[0], me[1], me[2]] = block16[:, g * 128 : (g + 1) * 128]
-    for part in PARTS:
-        for k in STEPS:
-            gather(part, 0, k).start()
-
+    for k, m in PLANE:
+        for part in PARTS:
+            scattered(part, k, m).start()
+
+    proj_half(1 - core)
+    pltpu.make_async_copy(cot, cot, load_sem.at[0]).wait()
+    peer_half(0)
     proj_half(core)
     peer_half(1)
     own_half(0)
     send_terms(0)
     peer_half(2)
-    for part in PARTS:
-        for k in STEPS:
-            gather(part, 0, k, True).wait_recv()
-    for part in PARTS:
-        for k in STEPS:
-            gather(part, 1, k).start()
     own_half(1)
     send_terms(1)
+    for part in PARTS:
+        settle(ag_send.at[part], ag_recv.at[part], 5, 3, 3).wait_recv()
+    for part in PARTS:
+        for k in (1, 3):
+            neighbour(part, k).start()
+    for part in PARTS:
+        forward(part, 0, core).start()
     peer_half(3)
     own_half(2)
     send_terms(2)
     own_half(3)
     send_terms(3)
+    combine_first(1)
+    combine(0)
     edge_load.wait()
     for i in range(OWN):
         u_acc[:, :, :, :, i * EDGE : (i + 1) * EDGE] = edge[i].astype(F32)
-    for part in PARTS:
-        for k in STEPS:
-            gather(part, 1, k, True).wait_recv()
-    for part in PARTS:
-        for k in (1, 3):
-            gather(part, 2, k).start()
-    for part in PARTS:
-        forward(part, 0, core).start()
 
     def scatter(part, phase, k):
         axes = axes_of(part)
@@ -295,30 +341,28 @@
         else:
             src, dst = sum2.at[groups, there], slab3.at[k - 1, groups]
         return remote(
-            src, dst, rs_send.at[part, phase - 1, k - 1], rs_recv.at[part, phase - 1, k - 1], device(to, core)
-        )
+            src, dst, rs_send.at[part, phase - 1], rs_recv.at[part, phase - 1], device(to, core)
+        )
+
+    def settled(part, phase):
+        send, recv = rs_send.at[part, phase - 1], rs_recv.at[part, phase - 1]
+        return settle(send, recv, 9 if part < 2 else 6, 4 if phase == 1 else 1, 1)
 
     def scatter_add(part, phase):
         axes = axes_of(part)
         here = me[axes[phase]]
         first_group, count = 3 * part, 3 if part < 2 else GROUPS - 6
         if phase == 0:
-            if part == 0:
-                for r in range(3):
-                    scatter_first(0, r, 0).wait_recv()
-            else:
-                for r in range(4):
-                    for k in STEPS:
-                        scatter_first(part, r, k).wait_recv()
+            sem, tiles = ((2, (6, 4, 4)), (7, (6, 4, 4)), (8, (4, 4, 4)))[part]
+            settle(r0_send.at[sem], r0_recv.at[sem], *tiles).wait_recv()
         else:
-            for k in STEPS:
-                scatter(part, phase, k).wait_recv()
+            settled(part, phase).wait_recv()
         for g in range(first_group, first_group + count):
             if phase == 0:
                 idx = [slice(None)] * 3
                 idx[axes[0]] = here
                 total = terms[g, idx[0], idx[1], idx[2]].astype(F32)
-                for k in range(3):
+                for k in range(2):
                     total += slab1[k, g].astype(F32)
                 sum1[g] = total.astype(BF16)
             elif phase == 1:
@@ -385,10 +429,7 @@
         u_acc[idx] = u_acc[idx] + u.reshape(4, 4, 16, OWN * EDGE)
 
     def forwarded(k):
-        for part in PARTS:
-            forward(part, k, 1 - core).wait_recv()
-            if k == 2:
-                forward(part, 4, 1 - core).wait_recv()
+        settle(fw_send.at[FORWARD[k]], fw_recv.at[FORWARD[k]], 9, 4, 4).wait_recv()
 
     def left_own(k):
         for part in PARTS:
@@ -403,16 +444,18 @@
             pair_plane(part, k)
 
     def neighbours():
+        for part in PARTS:
+            settle(nb_send.at[part], nb_recv.at[part], 6, 4, 4).wait_recv()
+            for k in (1, 3):
+                opposite(part, int(k == 3)).start()
         for k in (1, 3):
             for part in PARTS:
-                gather(part, 2, k, True).wait_recv()
-                opposite(part, int(k == 3)).start()
                 forward(part, k, core).start()
 
     def opposites():
         for part in PARTS:
+            settle(op_send.at[part], op_recv.at[part], 3, 4, 4).wait_recv()
             for upper in (0, 1):
-                opposite(part, upper, True).wait_recv()
                 forward(part, 2 + 2 * upper, core).start()
 
     def reduce(phase):
@@ -428,9 +471,13 @@
         gn_ref[...] = jnp.dot(grad_s[...].astype(BF16), w1t_ref[...], preferred_element_type=F32)
 
     left_own(0)
+    combine(1)
+    combine_first(2)
     forwarded(0)
     left_other(0)
+    combine(2)
     pair(0)
+    combine(3)
     neighbours()
     left_own(1)
     left_own(3)
@@ -472,44 +519,46 @@
     blk_copy.wait_send()
     fin_copy.wait_send()
     for part in PARTS:
-        for k in STEPS:
-            for phase in (1, 2):
-                scatter(part, phase, k).wait_send()
-            gather(part, 0, k).wait_send()
-            gather(part, 1, k).wait_send()
-        for k in (1, 3):
-            gather(part, 2, k).wait_send()
-        for upper in (0, 1):
-            opposite(part, upper).wait_send()
-        for k in range(5):
-            forward(part, k, core).wait_send()
+        for phase in (1, 2):
+            settled(part, phase).wait_send()
+        settle(ag_send.at[part], ag_recv.at[part], 5, 3, 3).wait_send()
+        settle(nb_send.at[part], nb_recv.at[part], 6, 4, 4).wait_send()
+        settle(op_send.at[part], op_recv.at[part], 3, 4, 4).wait_send()
+    for k in range(4):
+        settle(fw_send.at[k], fw_recv.at[k], 9, 4, 4).wait_send()
     for r in range(4):
-        if r < 3:
-            scatter_first(0, r, 0).wait_send()
-        for part in (1, 2):
-            for k in STEPS:
-                scatter_first(part, r, k).wait_send()
+        settle(r0_send.at[3 + r], r0_recv.at[3 + r], 5, 4, 1).wait_send()
         peer_copy(r).wait_send()
+    for sem, tiles in ((2, (6, 4, 4)), (7, (6, 4, 4)), (8, (4, 4, 4))):
+        settle(r0_send.at[sem], r0_recv.at[sem], *tiles).wait_send()
+    for upper in (0, 1):
+        hop_first(upper).wait_send()
 
 
 def finish_kernel(
     u_ref, labels, gn_ref, unit_ref, rstd_ref, gain_ref, off_ref, smo_ref, pad_ref, mol_ref,
     pair_out, grad_out, held, grad, sems,
 ):
-    stores = [pltpu.make_async_copy(held.at[i], pair_out.at[i], sems.at[i]) for i in range(OWN)]
-    grad_store = pltpu.make_async_copy(grad, grad_out, sems.at[OWN])
-    keep_j = labels[0].astype(F32)
-    mol_j = labels[1].astype(F32)
-    apart = keep_j * off_ref[...]
-    together = keep_j * (off_ref[...] + smo_ref[...])
-
-    def pair(i):
-        extra = jnp.where(mol_j == mol_ref[i].astype(F32), together, apart) * pad_ref[i].astype(F32)
-        held[i] = (u_ref[:, i * EDGE : (i + 1) * EDGE] + extra).astype(BF16)
-        stores[i].start()
-
-    for i in range(4):
-        pair(i)
+    def store(q):
+        rows = pl.ds(q * 256, 256)
+        return pltpu.make_async_copy(held.at[:, rows], pair_out.at[:, rows], sems.at[q])
+
+    grad_store = pltpu.make_async_copy(grad, grad_out, sems.at[4])
+
+    def pair(q):
+        for lo in range(q * 256, q * 256 + 256, 64):
+            rows = slice(lo, lo + 64)
+            keep_j = labels[0, rows, :].astype(F32)
+            mol_j = labels[1, rows, :].astype(F32)
+            apart = keep_j * off_ref[...]
+            together = keep_j * (off_ref[...] + smo_ref[...])
+            for i in range(OWN):
+                extra = jnp.where(mol_j == mol_ref[i].astype(F32), together, apart) * pad_ref[i].astype(F32)
+                held[i, rows, :] = (u_ref[rows, i * EDGE : (i + 1) * EDGE] + extra).astype(BF16)
+        store(q).start()
+
+    pair(0)
+    pair(1)
     unit = unit_ref[...]
     gained = gn_ref[...] * gain_ref[...]
     result = rstd_ref[:, :1] * (
@@ -519,10 +568,10 @@
     )
     grad[...] = result.reshape(SEQS, OWN, FEAT)
     grad_store.start()
-    for i in range(4, OWN):
-        pair(i)
-    for cp in stores:
-        cp.wait()
+    pair(2)
+    pair(3)
+    for q in range(4):
+        store(q).wait()
     grad_store.wait()
 
 
@@ -562,7 +611,9 @@
             pltpu.VMEM((GROUPS, 4, 4, 4, 16, 128), BF16),
             pltpu.VMEM((4, 256, HALF), BF16),
             pltpu.VMEM((4, 256, HALF), BF16),
-            pltpu.VMEM((3, GROUPS, 4, 4, 16, 128), BF16),
+            pltpu.VMEM((2, 3, 2, 4, 16, 128), BF16),
+            pltpu.VMEM((2, 4, GROUPS, 4, 16, 128), BF16),
+            pltpu.VMEM((2, GROUPS, 4, 4, 16, 128), BF16),
             pltpu.VMEM((GROUPS, 4, 4, 16, 128), BF16),
             pltpu.VMEM((3, GROUPS, 4, 16, 128), BF16),
             pltpu.VMEM((GROUPS, 4, 16, 128), BF16),
@@ -578,17 +629,19 @@
             pltpu.VMEM((16, HALF), F32),
             pltpu.VMEM((OWN, HALF), F32),
             pltpu.VMEM((OWN, HALF), F32),
-            dma((OWN + 8,)),
-            dma((3, 3, 3)),
-            dma((3, 3, 3)),
+            dma((9,)),
+            dma((3,)),
+            dma((3,)),
+            dma((3,)),
+            dma((3,)),
+            dma((3,)),
+            dma((3,)),
+            dma((4,)),
+            dma((4,)),
+            dma((9,)),
+            dma((9,)),
             dma((3, 2)),
             dma((3, 2)),
-            dma((3, 5)),
-            dma((3, 5)),
-            dma((3, 4, 3)),
-            dma((3, 4, 3)),
-            dma((3, 2, 3)),
-            dma((3, 2, 3)),
             dma((4,)),
             dma((4,)),
             dma((2,)),
@@ -610,7 +663,7 @@
         scratch_shapes=[
             pltpu.VMEM((OWN, LENGTH, EDGE), BF16),
             pltpu.VMEM((SEQS, OWN, FEAT), F32),
-            dma((OWN + 1,)),
+            dma((5,)),
         ],
         compiler_params=pltpu.CompilerParams(vmem_limit_bytes=16 * 2**20),
         name="finish",

time: 49.9 us -> 46.1 us (0.924)
  Pallas kernels: 48.9 us -> 45 us
    pallas_call x1, Pallas kernels: 45.3 us -> 42.5 us  [local(): pl.pallas_call(exchange_kernel, out_shape=(pltpu.VMEM((4, 4, 4, 16, OWN *...]
    pallas_call x1, Pallas kernels: 3.55 us -> 2.57 us  [local(): pl.pallas_call(finish_kernel, out_shape=(jax.ShapeDtypeStruct(edge.shape,...]
where the time goes in v3:
time: 46.1 us; the launch traced here: 46 us
  Pallas kernels  45 us (98%)
  between operations  0.9 us (2%)
    pallas_call x1, Pallas kernels, local(): pl.pallas_call(exchange_kernel, out_shape=(pltpu.VMEM((4, 4, 4, 16, OWN *...  42.5 us
    pallas_call x1, Pallas kernels, local(): pl.pallas_call(finish_kernel, out_shape=(jax.ShapeDtypeStruct(edge.shape,...  2.57 us

profile of v3, /device:TPU:1, one launch (start us, length us, event | category | flops | bytes accessed | tf_op | source)
XLA Modules:
  0.0 46.0 jit_solution(10820226043908179671)
XLA Ops:
  0.6 0.0 copy-start
  0.6 0.0 copy-start.1
  0.7 0.0 copy-start.2
  0.7 0.0 copy-start.3
  0.7 0.0 copy-start.4
  0.7 42.5 %outer_product_mean.1 = (f32[4,4,4,16,1024]{4,3,2,1,0:T(8,128)S(1)}, bf16[2,4,4,4,16,128]{5,4,3,2,1,0:T(8,128)(2,1)S(1)}, f32[512,256]{1,0:T(8,128)S(1)}, f32[512,256]{1,0:T(8,128)S(1)}, f32[512,128]{1,0:T(8,128)S(1)}) custom-call(bf16[64,8,256]{2,1,0:T(8,128)(2,1)} %x_hbm.1, f32[1,256]{1,0:T(1,128)} %bitcast.11, bf16[32,256]{1,0:T(8,128)(2,1)} %bitcast.17, ...), custom_call_target="tpu_custom_call" | custom-call | tf_op jit(solution)/shard_map/outer_product_mean/pallas_call | solution.py:587
  43.2 0.0 copy-done
  43.2 0.0 copy-done.1
  43.2 0.0 copy-done.2
  43.2 0.0 copy-done.3
  43.2 0.0 copy-done.4
  43.2 2.6 %finish.1 = (bf16[8,1024,128]{2,1,0:T(8,128)(2,1)}, f32[64,8,256]{2,1,0:T(8,128)}) custom-call(f32[1024,1024]{1,0:T(8,128)S(1)} %bitcast.9, bf16[2,1024,128]{2,1,0:T(8,128)(2,1)S(1)} %bitcast.10, f32[512,256]{1,0:T(8,128)S(1)} %get-tuple-element.9.gn_ref, f32[512,256]{1,0:T(8,128)S(1)} %get-tuple-element.10.unit_ref, ...), custom_call_target="tpu_custom_call" | custom-call | tf_op jit(solution)/shard_map/finish/pallas_call | solution.py:655
Async XLA Ops:
  0.6 42.5 %copy-start = (f32[256]{0:T(256)S(1)}, f32[256]{0:T(256)}, u32[]{:S(2)}) copy-start(f32[256]{0:T(256)} %param.12) | copy-start | bytes 3076
  0.6 42.5 %copy-start.1 = (s32[8]{0:T(128)S(1)}, s32[8]{0:T(128)}, u32[]{:S(2)}) copy-start(s32[8]{0:T(128)} %pad_ref.1) | copy-start | bytes 100
  0.7 42.5 %copy-start.2 = (s32[8]{0:T(128)S(1)}, s32[8]{0:T(128)}, u32[]{:S(2)}) copy-start(s32[8]{0:T(128)} %mol_ref.1) | copy-start | bytes 100
  0.7 42.5 %copy-start.3 = (f32[128]{0:T(128)S(1)}, f32[128]{0:T(128)}, u32[]{:S(2)}) copy-start(f32[128]{0:T(128)} %param.16) | copy-start | bytes 1540
  0.7 42.5 %copy-start.4 = (f32[128]{0:T(128)S(1)}, f32[128]{0:T(128)}, u32[]{:S(2)}) copy-start(f32[128]{0:T(128)} %param.17) | copy-start | bytes 1540

commit v4 on v3

--- a/solution.py
+++ b/solution.py
@@ -22,6 +22,7 @@
 PARTS = (0, 1, 2)
 STEPS = (1, 2, 3)
 FORWARD = (0, 1, 3, 2, 3)
+DIRECT = (2, 3)
 PLANE = tuple((k, m) for k in range(4) for m in range(4) if k or m)
 
 
@@ -138,35 +139,34 @@
     blk_out[...] = jnp.where(first, half1, half0)
     own_blk = jnp.where(first, half0, half1)
 
-    pl.semaphore_wait(barrier, 37)
-    blk_copy = remote(blk_out, blk_in, misc_send.at[0], misc_recv.at[0], sibling)
-    blk_copy.start()
-
     left_s[...] = nt(normed, w1t_ref[...]).astype(BF16).astype(F32)
     wff[...] = wf_ref[...].astype(F32)
     for b in range(FACTOR):
         wflat[:, b * EDGE : (b + 1) * EDGE] = wff[pl.ds(b, FACTOR, stride=FACTOR), :].astype(BF16)
     for i in range(OWN):
         rows = left_s[pl.ds(i, SEQS, stride=OWN), :] * (pad_ref[i].astype(F32) * (1.0 / SEQS))
-        for half in range(2):
-            left_b[half, i * 32 : i * 32 + 32, :] = rows[half * 32 : half * 32 + 32].astype(BF16)
-
-    def proj_half(half):
-        left = left_b[half]
+        left_b[i * SEQS : (i + 1) * SEQS, :] = rows.astype(BF16)
+
+    def proj_steps(start, stop):
+        left = left_b[...]
 
         def step(m, carry):
             for v in range(4):
                 n = m * 4 + v
                 y = jnp.dot(left, wflat[:, pl.ds(pl.multiple_of(n * 256, 256), 256)], preferred_element_type=F32)
                 for i in range(OWN):
-                    for h in range(4):
-                        tile = y[i * 32 + h * 8 : i * 32 + h * 8 + 8]
+                    for h in range(8):
+                        tile = y[i * SEQS + h * 8 : i * SEQS + h * 8 + 8]
                         pair = jnp.concatenate([tile[:, :EDGE], tile[:, EDGE:]], axis=0).astype(BF16)
-                        top = pl.multiple_of(half * HALF + h * 256 + n * 16, 16)
+                        top = pl.multiple_of(h * 256 + n * 16, 16)
                         proj[pl.ds(top, 16), i * EDGE : (i + 1) * EDGE] = pair
             return carry
 
-        lax.fori_loop(0, 4, step, 0)
+        lax.fori_loop(start, stop, step, 0)
+
+    pl.semaphore_wait(barrier, 37)
+    blk_copy = remote(blk_out, blk_in, misc_send.at[0], misc_recv.at[0], sibling)
+    blk_copy.start()
 
     def plane_index(part, phase, at):
         idx = list(at)
@@ -247,7 +247,7 @@
         sem = 3 + r if what == 0 else 6 + part
         return remote(
             src, dst, r0_send.at[sem], r0_recv.at[sem],
-            device(shifted(part, 1 if up else 3), core),
+            device(there if what == 0 and r in DIRECT else shifted(part, 1 if up else 3), core),
         )
 
     def combine(r):
@@ -281,6 +281,8 @@
         for part in (1, 2):
             scatter_first(part, r, 0).start()
             scatter_first(part, r, 2 if r % 2 == 0 else 1).start()
+            if r in DIRECT:
+                scatter_first(part, r, 1 if r % 2 == 0 else 2).start()
 
     def combine_first(r):
         upper = r - 1
@@ -290,6 +292,7 @@
             terms[idx] = (terms[idx].astype(F32) + hop0[upper, g].astype(F32)).astype(BF16)
         slab_first(r).start()
 
+    proj_steps(0, 2)
     blk_copy.wait_recv()
     theirs = blk_in[...]
     block16 = jnp.concatenate(
@@ -301,16 +304,16 @@
         for part in PARTS:
             scattered(part, k, m).start()
 
-    proj_half(1 - core)
+    proj_steps(2, 4)
     pltpu.make_async_copy(cot, cot, load_sem.at[0]).wait()
     peer_half(0)
-    proj_half(core)
     peer_half(1)
     own_half(0)
     send_terms(0)
     peer_half(2)
     own_half(1)
     send_terms(1)
+    peer_half(3)
     for part in PARTS:
         settle(ag_send.at[part], ag_recv.at[part], 5, 3, 3).wait_recv()
     for part in PARTS:
@@ -318,7 +321,6 @@
             neighbour(part, k).start()
     for part in PARTS:
         forward(part, 0, core).start()
-    peer_half(3)
     own_half(2)
     send_terms(2)
     own_half(3)
@@ -358,6 +360,11 @@
         else:
             settled(part, phase).wait_recv()
         for g in range(first_group, first_group + count):
+            if phase == 0 and part > 0:
+                for r in DIRECT:
+                    q = quarter(r)
+                    late = slab1[0, g, q].astype(F32) + hop[part - 1, q, g].astype(F32)
+                    slab1[0, g, q] = late.astype(BF16)
             if phase == 0:
                 idx = [slice(None)] * 3
                 idx[axes[0]] = here
@@ -459,6 +466,9 @@
                 forward(part, 2 + 2 * upper, core).start()
 
     def reduce(phase):
+        if phase == 0:
+            for r in DIRECT:
+                settle(r0_send.at[3 + r], r0_recv.at[3 + r], 5, 4, 1).wait_recv()
         for part in PARTS:
             scatter_add(part, phase)
 
@@ -475,15 +485,13 @@
     combine_first(2)
     forwarded(0)
     left_other(0)
-    combine(2)
     pair(0)
-    combine(3)
     neighbours()
     left_own(1)
     left_own(3)
-    reduce(0)
     forwarded(1)
     left_other(1)
+    reduce(0)
     forwarded(3)
     left_other(3)
     opposites()
@@ -606,7 +614,7 @@
             pltpu.VMEM((OWN, 4, 4, 4, 16, EDGE), BF16),
             pltpu.VMEM((4, 4, 4, 16, OWN * EDGE), BF16),
             pltpu.VMEM((2, GROUPS + 1, 4, 4, 4, 16, 128), BF16),
-            pltpu.VMEM((2, OWN * 32, FACTOR), BF16),
+            pltpu.VMEM((SEQS * OWN, FACTOR), BF16),
             pltpu.VMEM((2 * HALF, OWN * EDGE), BF16),
             pltpu.VMEM((GROUPS, 4, 4, 4, 16, 128), BF16),
             pltpu.VMEM((4, 256, HALF), BF16),

time: 46.1 us -> 44.9 us (0.974)
  Pallas kernels: 45 us -> 43.8 us
    pallas_call x1, Pallas kernels: 42.5 us -> 41.3 us  [local(): pl.pallas_call(exchange_kernel, out_shape=(pltpu.VMEM((4, 4, 4, 16, OWN *...]
where the time goes in v4:
time: 44.9 us; the launch traced here: 44.8 us
  Pallas kernels  43.8 us (98%)
  between operations  0.9 us (2%)
    pallas_call x1, Pallas kernels, local(): pl.pallas_call(exchange_kernel, out_shape=(pltpu.VMEM((4, 4, 4, 16, OWN *...  41.3 us
    pallas_call x1, Pallas kernels, local(): pl.pallas_call(finish_kernel, out_shape=(jax.ShapeDtypeStruct(edge.shape,...  2.57 us

profile of v4, /device:TPU:1, one launch (start us, length us, event | category | flops | bytes accessed | tf_op | source)
XLA Modules:
  0.0 44.8 jit_solution(4181619815429298270)
XLA Ops:
  0.6 0.0 copy-start
  0.6 0.0 copy-start.1
  0.7 0.0 copy-start.2
  0.7 0.0 copy-start.3
  0.7 0.0 copy-start.4
  0.7 41.3 %outer_product_mean.1 = (f32[4,4,4,16,1024]{4,3,2,1,0:T(8,128)S(1)}, bf16[2,4,4,4,16,128]{5,4,3,2,1,0:T(8,128)(2,1)S(1)}, f32[512,256]{1,0:T(8,128)S(1)}, f32[512,256]{1,0:T(8,128)S(1)}, f32[512,128]{1,0:T(8,128)S(1)}) custom-call(bf16[64,8,256]{2,1,0:T(8,128)(2,1)} %x_hbm.1, f32[1,256]{1,0:T(1,128)} %bitcast.11, bf16[32,256]{1,0:T(8,128)(2,1)} %bitcast.17, ...), custom_call_target="tpu_custom_call" | custom-call | tf_op jit(solution)/shard_map/outer_product_mean/pallas_call | solution.py:595
  42.0 0.0 copy-done
  42.0 0.0 copy-done.1
  42.0 0.0 copy-done.2
  42.0 0.0 copy-done.3
  42.0 0.0 copy-done.4
  42.0 2.6 %finish.1 = (bf16[8,1024,128]{2,1,0:T(8,128)(2,1)}, f32[64,8,256]{2,1,0:T(8,128)}) custom-call(f32[1024,1024]{1,0:T(8,128)S(1)} %bitcast.9, bf16[2,1024,128]{2,1,0:T(8,128)(2,1)S(1)} %bitcast.10, f32[512,256]{1,0:T(8,128)S(1)} %get-tuple-element.9.gn_ref, f32[512,256]{1,0:T(8,128)S(1)} %get-tuple-element.10.unit_ref, ...), custom_call_target="tpu_custom_call" | custom-call | tf_op jit(solution)/shard_map/finish/pallas_call | solution.py:663
Async XLA Ops:
  0.6 41.3 %copy-start = (f32[256]{0:T(256)S(1)}, f32[256]{0:T(256)}, u32[]{:S(2)}) copy-start(f32[256]{0:T(256)} %param.12) | copy-start | bytes 3076
  0.6 41.3 %copy-start.1 = (s32[8]{0:T(128)S(1)}, s32[8]{0:T(128)}, u32[]{:S(2)}) copy-start(s32[8]{0:T(128)} %pad_ref.1) | copy-start | bytes 100
  0.7 41.3 %copy-start.2 = (s32[8]{0:T(128)S(1)}, s32[8]{0:T(128)}, u32[]{:S(2)}) copy-start(s32[8]{0:T(128)} %mol_ref.1) | copy-start | bytes 100
  0.7 41.3 %copy-start.3 = (f32[128]{0:T(128)S(1)}, f32[128]{0:T(128)}, u32[]{:S(2)}) copy-start(f32[128]{0:T(128)} %param.16) | copy-start | bytes 1540
  0.7 41.3 %copy-start.4 = (f32[128]{0:T(128)S(1)}, f32[128]{0:T(128)}, u32[]{:S(2)}) copy-start(f32[128]{0:T(128)} %param.17) | copy-start | bytes 1540

commit v5 on v4

--- a/solution.py
+++ b/solution.py
@@ -308,12 +308,14 @@
     pltpu.make_async_copy(cot, cot, load_sem.at[0]).wait()
     peer_half(0)
     peer_half(1)
+    peer_half(2)
     own_half(0)
     send_terms(0)
-    peer_half(2)
     own_half(1)
     send_terms(1)
     peer_half(3)
+    own_half(2)
+    send_terms(2)
     for part in PARTS:
         settle(ag_send.at[part], ag_recv.at[part], 5, 3, 3).wait_recv()
     for part in PARTS:
@@ -321,8 +323,6 @@
             neighbour(part, k).start()
     for part in PARTS:
         forward(part, 0, core).start()
-    own_half(2)
-    send_terms(2)
     own_half(3)
     send_terms(3)
     combine_first(1)

time: 44.9 us -> 44.1 us (0.982)
  Pallas kernels: 43.8 us -> 43 us
    pallas_call x1, Pallas kernels: 41.3 us -> 40.4 us  [local(): pl.pallas_call(exchange_kernel, out_shape=(pltpu.VMEM((4, 4, 4, 16, OWN *...]
where the time goes in v5:
time: 44.1 us; the launch traced here: 43.9 us
  Pallas kernels  43 us (98%)
  between operations  0.9 us (2%)
    pallas_call x1, Pallas kernels, local(): pl.pallas_call(exchange_kernel, out_shape=(pltpu.VMEM((4, 4, 4, 16, OWN *...  40.4 us
    pallas_call x1, Pallas kernels, local(): pl.pallas_call(finish_kernel, out_shape=(jax.ShapeDtypeStruct(edge.shape,...  2.57 us

profile of v5, /device:TPU:1, one launch (start us, length us, event | category | flops | bytes accessed | tf_op | source)
XLA Modules:
  0.0 43.9 jit_solution(1303605739037792295)
XLA Ops:
  0.6 0.0 copy-start
  0.6 0.0 copy-start.1
  0.7 0.0 copy-start.2
  0.7 0.0 copy-start.3
  0.7 0.0 copy-start.4
  0.7 40.4 %outer_product_mean.1 = (f32[4,4,4,16,1024]{4,3,2,1,0:T(8,128)S(1)}, bf16[2,4,4,4,16,128]{5,4,3,2,1,0:T(8,128)(2,1)S(1)}, f32[512,256]{1,0:T(8,128)S(1)}, f32[512,256]{1,0:T(8,128)S(1)}, f32[512,128]{1,0:T(8,128)S(1)}) custom-call(bf16[64,8,256]{2,1,0:T(8,128)(2,1)} %x_hbm.1, f32[1,256]{1,0:T(1,128)} %bitcast.11, bf16[32,256]{1,0:T(8,128)(2,1)} %bitcast.17, ...), custom_call_target="tpu_custom_call" | custom-call | tf_op jit(solution)/shard_map/outer_product_mean/pallas_call | solution.py:595
  41.1 0.0 copy-done
  41.1 0.0 copy-done.1
  41.2 0.0 copy-done.2
  41.2 0.0 copy-done.3
  41.2 0.0 copy-done.4
  41.2 2.6 %finish.1 = (bf16[8,1024,128]{2,1,0:T(8,128)(2,1)}, f32[64,8,256]{2,1,0:T(8,128)}) custom-call(f32[1024,1024]{1,0:T(8,128)S(1)} %bitcast.9, bf16[2,1024,128]{2,1,0:T(8,128)(2,1)S(1)} %bitcast.10, f32[512,256]{1,0:T(8,128)S(1)} %get-tuple-element.9.gn_ref, f32[512,256]{1,0:T(8,128)S(1)} %get-tuple-element.10.unit_ref, ...), custom_call_target="tpu_custom_call" | custom-call | tf_op jit(solution)/shard_map/finish/pallas_call | solution.py:663
Async XLA Ops:
  0.6 40.5 %copy-start = (f32[256]{0:T(256)S(1)}, f32[256]{0:T(256)}, u32[]{:S(2)}) copy-start(f32[256]{0:T(256)} %param.12) | copy-start | bytes 3076
  0.6 40.5 %copy-start.1 = (s32[8]{0:T(128)S(1)}, s32[8]{0:T(128)}, u32[]{:S(2)}) copy-start(s32[8]{0:T(128)} %pad_ref.1) | copy-start | bytes 100
  0.7 40.5 %copy-start.2 = (s32[8]{0:T(128)S(1)}, s32[8]{0:T(128)}, u32[]{:S(2)}) copy-start(s32[8]{0:T(128)} %mol_ref.1) | copy-start | bytes 100
  0.7 40.5 %copy-start.3 = (f32[128]{0:T(128)S(1)}, f32[128]{0:T(128)}, u32[]{:S(2)}) copy-start(f32[128]{0:T(128)} %param.16) | copy-start | bytes 1540
  0.7 40.5 %copy-start.4 = (f32[128]{0:T(128)S(1)}, f32[128]{0:T(128)}, u32[]{:S(2)}) copy-start(f32[128]{0:T(128)} %param.17) | copy-start | bytes 1540

commit v6 on v5

--- a/solution.py
+++ b/solution.py
@@ -548,13 +548,13 @@
     pair_out, grad_out, held, grad, sems,
 ):
     def store(q):
-        rows = pl.ds(q * 256, 256)
+        rows = pl.ds(q * 128, 128)
         return pltpu.make_async_copy(held.at[:, rows], pair_out.at[:, rows], sems.at[q])
 
-    grad_store = pltpu.make_async_copy(grad, grad_out, sems.at[4])
+    grad_store = pltpu.make_async_copy(grad, grad_out, sems.at[8])
 
     def pair(q):
-        for lo in range(q * 256, q * 256 + 256, 64):
+        for lo in range(q * 128, q * 128 + 128, 64):
             rows = slice(lo, lo + 64)
             keep_j = labels[0, rows, :].astype(F32)
             mol_j = labels[1, rows, :].astype(F32)
@@ -565,8 +565,8 @@
                 held[i, rows, :] = (u_ref[rows, i * EDGE : (i + 1) * EDGE] + extra).astype(BF16)
         store(q).start()
 
-    pair(0)
-    pair(1)
+    for q in range(4):
+        pair(q)
     unit = unit_ref[...]
     gained = gn_ref[...] * gain_ref[...]
     result = rstd_ref[:, :1] * (
@@ -576,9 +576,9 @@
     )
     grad[...] = result.reshape(SEQS, OWN, FEAT)
     grad_store.start()
-    pair(2)
-    pair(3)
-    for q in range(4):
+    for q in range(4, 8):
+        pair(q)
+    for q in range(8):
         store(q).wait()
     grad_store.wait()
 
@@ -671,7 +671,7 @@
         scratch_shapes=[
             pltpu.VMEM((OWN, LENGTH, EDGE), BF16),
             pltpu.VMEM((SEQS, OWN, FEAT), F32),
-            dma((5,)),
+            dma((9,)),
         ],
         compiler_params=pltpu.CompilerParams(vmem_limit_bytes=16 * 2**20),
         name="finish",

time: 44.1 us -> 44 us (level)
  no operation moved by 1% of the time
where the time goes in v6:
time: 44 us; the launch traced here: 43.9 us
  Pallas kernels  43 us (98%)
  between operations  0.9 us (2%)
    pallas_call x1, Pallas kernels, local(): pl.pallas_call(exchange_kernel, out_shape=(pltpu.VMEM((4, 4, 4, 16, OWN *...  40.4 us
    pallas_call x1, Pallas kernels, local(): pl.pallas_call(finish_kernel, out_shape=(jax.ShapeDtypeStruct(edge.shape,...  2.51 us

profile of v6, /device:TPU:1, one launch (start us, length us, event | category | flops | bytes accessed | tf_op | source)
XLA Modules:
  0.0 43.9 jit_solution(4096001339349701124)
XLA Ops:
  0.6 0.0 copy-start
  0.6 0.0 copy-start.1
  0.7 0.0 copy-start.2
  0.7 0.0 copy-start.3
  0.7 0.0 copy-start.4
  0.7 40.4 %outer_product_mean.1 = (f32[4,4,4,16,1024]{4,3,2,1,0:T(8,128)S(1)}, bf16[2,4,4,4,16,128]{5,4,3,2,1,0:T(8,128)(2,1)S(1)}, f32[512,256]{1,0:T(8,128)S(1)}, f32[512,256]{1,0:T(8,128)S(1)}, f32[512,128]{1,0:T(8,128)S(1)}) custom-call(bf16[64,8,256]{2,1,0:T(8,128)(2,1)} %x_hbm.1, f32[1,256]{1,0:T(1,128)} %bitcast.11, bf16[32,256]{1,0:T(8,128)(2,1)} %bitcast.17, ...), custom_call_target="tpu_custom_call" | custom-call | tf_op jit(solution)/shard_map/outer_product_mean/pallas_call | solution.py:595
  41.1 0.0 copy-done
  41.1 0.0 copy-done.1
  41.2 0.0 copy-done.2
  41.2 0.0 copy-done.3
  41.2 0.0 copy-done.4
  41.2 2.5 %finish.1 = (bf16[8,1024,128]{2,1,0:T(8,128)(2,1)}, f32[64,8,256]{2,1,0:T(8,128)}) custom-call(f32[1024,1024]{1,0:T(8,128)S(1)} %bitcast.9, bf16[2,1024,128]{2,1,0:T(8,128)(2,1)S(1)} %bitcast.10, f32[512,256]{1,0:T(8,128)S(1)} %get-tuple-element.9.gn_ref, f32[512,256]{1,0:T(8,128)S(1)} %get-tuple-element.10.unit_ref, ...), custom_call_target="tpu_custom_call" | custom-call | tf_op jit(solution)/shard_map/finish/pallas_call | solution.py:663
Async XLA Ops:
  0.6 40.5 %copy-start = (f32[256]{0:T(256)S(1)}, f32[256]{0:T(256)}, u32[]{:S(2)}) copy-start(f32[256]{0:T(256)} %param.12) | copy-start | bytes 3076
  0.6 40.5 %copy-start.1 = (s32[8]{0:T(128)S(1)}, s32[8]{0:T(128)}, u32[]{:S(2)}) copy-start(s32[8]{0:T(128)} %pad_ref.1) | copy-start | bytes 100
  0.7 40.5 %copy-start.2 = (s32[8]{0:T(128)S(1)}, s32[8]{0:T(128)}, u32[]{:S(2)}) copy-start(s32[8]{0:T(128)} %mol_ref.1) | copy-start | bytes 100
  0.7 40.5 %copy-start.3 = (f32[128]{0:T(128)S(1)}, f32[128]{0:T(128)}, u32[]{:S(2)}) copy-start(f32[128]{0:T(128)} %param.16) | copy-start | bytes 1540
  0.7 40.5 %copy-start.4 = (f32[128]{0:T(128)S(1)}, f32[128]{0:T(128)}, u32[]{:S(2)}) copy-start(f32[128]{0:T(128)} %param.17) | copy-start | bytes 1540
